TPU v7x, 128 devices: a whole 4x4x4 slice. The times are simulated.
128 devices in a mesh: zonal: 16 (over z_lo, y, core), merid: 8 (over x, z_hi).
Axes of the slice: x: 4, y: 4, z: 4 (z_hi: 2, z_lo: 2; z = z_hi * 2 + z_lo), core: 2. Of those that a mesh axis runs over, the one named last changes fastest.
Arguments:
- field: bfloat16 [200, 128, 2048], P(None, 'merid', 'zonal'), may hold values from -6 to 6
- land_mask: int32 [128, 2048], P('merid', 'zonal'), may hold values 0 or 1
- fold_partner: int32 [2048], replicated, may hold values from 0 to 2047, as said below
- dw_kernel: bfloat16 [3, 200, 7, 7], replicated, may hold values from -0.875 to 0.875
- norm_gain: bfloat16 [3, 200], replicated, may hold values from 0.25 to 1.75
- w_in: bfloat16 [3, 200, 800], replicated, may hold values from -0.4375 to 0.4375
- w_out: bfloat16 [3, 800, 200], replicated, may hold values from -0.21875 to 0.21875
Outputs:
- state: bfloat16 [200, 128, 2048], P(None, 'merid', 'zonal')
Inputs may be any that keep to these rules, and one draw needn't show every extreme that they name: fold_partner[j] = (s - j) mod 2048 for one s.
All inputs are finite; a program needn't handle non-finite values. No bound on the sum of `land_mask` on one device may be relied on, other than what follows from the above.
Results may differ from a plain program's by a relative error of at most 0.012.
Values may be sent and summed in bfloat16 or wider, within the bound.
No kernel may reach another device: no remote copies, remote signals or barrier semaphores. Data moves between devices by JAX's collectives and lax.ppermute only.
A program may use at most 128 MiB of HBM per device.

v0:
```python
import jax
import jax.numpy as jnp
import numpy as np
from jax import lax
from jax.experimental import pallas as pl
from jax.experimental.pallas import tpu as pltpu
from jax.sharding import PartitionSpec as P

BLOCKS = 3
C = 200
PAD = 208
H = 800
ROWS = 16
LANES = 128
GROUPS = C // 8
MAIN = 8 * ROWS
SIDE = 8 * 6
EPS = 1e-05
F32 = jnp.float32
BF16 = jnp.bfloat16
EDGE_ROWS = (0, 1, 2, 13, 14, 15)
PACK = 40
SEND = PAD + 3 * C + 2 * PACK + 8
SWAP = 3 * C + PACK
BOT = 3 * C + 8
VM = pl.BlockSpec(memory_space=pltpu.VMEM)
SM = pl.BlockSpec(memory_space=pltpu.SMEM)
ANY = pl.BlockSpec(memory_space=pl.ANY)


def dot32(a, b):
    return jnp.dot(a, b, preferred_element_type=F32)


def lanes_bf16(rows):
    return lax.broadcasted_iota(jnp.int32, (rows, LANES), 1).astype(F32).astype(BF16)


def pack_corner(v):
    lane = lax.broadcasted_iota(jnp.int32, (PACK, LANES), 1)
    packed = v[:PACK]
    for q in range(1, C // PACK):
        packed = jnp.where(lane >= 24 * q, pltpu.roll(v[PACK * q : PACK * (q + 1)], 24 * q, 1), packed)
    return packed


def band_kernel(block, taps_ref, w_in_ref, gain_ref, main_ref, side_ref, w1_ref, gains_ref):
    rows = [jnp.concatenate([taps_ref[block, a].astype(F32), jnp.zeros((1, C), F32)], axis=0) for a in range(7)]
    taps = jnp.concatenate(rows + [jnp.zeros((8, C), F32)], axis=0).T.astype(BF16)

    def place(first, second, tap_of, own, out_ref, at):
        depth = own.shape[1]
        tap = lax.broadcasted_iota(jnp.int32, (64, depth), 0)
        both = []
        for i in (first, second):
            spread = jnp.where(tap == tap_of(i), 1.0, 0.0).astype(BF16)
            both.append(dot32(taps, spread).reshape(GROUPS, 8, depth))
        both = jnp.concatenate(both, axis=1).astype(BF16)
        out_ref[:, pl.ds(at, 16), :] = both * own[None]

    lane = lax.broadcasted_iota(jnp.int32, (1, 7 * MAIN), 1)
    e, row = lane // MAIN, lane % ROWS

    def main_tap(i):
        a = row + 3 - i
        return jnp.where((a >= 0) & (a < 7), 8 * a + e, -1)

    wide = lax.broadcasted_iota(jnp.int32, (16, 7 * MAIN), 1)
    high = lax.broadcasted_iota(jnp.int32, (16, 7 * MAIN), 0)
    own_main = jnp.where((wide % MAIN) // ROWS == high % 8, 1.0, 0.0).astype(BF16)

    def main_pair(p, carry):
        place(2 * p, 2 * p + 1, main_tap, own_main, main_ref, pl.multiple_of(16 * p, 16))
        return carry

    lax.fori_loop(0, ROWS // 2, main_pair, 0, unroll=4)
    lane = lax.broadcasted_iota(jnp.int32, (1, 7 * SIDE), 1)
    e_side, slot = lane // SIDE, lane % SIDE
    k = slot // 8
    row_side = jnp.where(k < 3, k, k + ROWS)

    def side_tap(i):
        a = row_side - i
        return jnp.where((a >= 0) & (a < 7), 8 * a + e_side, -1)

    wide = lax.broadcasted_iota(jnp.int32, (16, 7 * SIDE), 1)
    high = lax.broadcasted_iota(jnp.int32, (16, 7 * SIDE), 0)
    own_side = jnp.where(wide % 8 == high % 8, 1.0, 0.0).astype(BF16)
    for p in range(3):
        place(EDGE_ROWS[2 * p], EDGE_ROWS[2 * p + 1], side_tap, own_side, side_ref, 16 * p)
    w1_ref[...] = w_in_ref[block].T
    gain = gain_ref[...].astype(F32)[block : block + 1]
    gains_ref[...] = jnp.broadcast_to(gain, (LANES, C)).T


def make_bands(block, taps, w_in, gain):
    return pl.pallas_call(
        lambda *refs: band_kernel(block, *refs),
        out_shape=(
            jax.ShapeDtypeStruct((GROUPS, MAIN, 7 * MAIN), BF16),
            jax.ShapeDtypeStruct((GROUPS, SIDE, 7 * SIDE), BF16),
            jax.ShapeDtypeStruct((H, C), BF16),
            jax.ShapeDtypeStruct((C, LANES), F32),
        ),
        in_specs=[VM] * 3,
        out_specs=(VM,) * 4,
        compiler_params=pltpu.CompilerParams(vmem_limit_bytes=14 * 2**20),
        cost_estimate=pl.CostEstimate(flops=2 * 16 * 256 * 256 * 1024, bytes_accessed=9_000_000, transcendentals=0),
    )(taps, w_in, gain)


def emit_edges(tile_of, o_ref, out_ref, send_ref, bot_ref):
    lane = lanes_bf16(ROWS)

    def some(first, count):
        v = tile_of(first, count)
        o_ref[pl.ds(first * ROWS, count * ROWS), :] = v.reshape(count * ROWS, LANES)
        v = v.astype(BF16)
        if out_ref is not None:
            out_ref[pl.ds(first, count)] = v
        packed = pltpu.roll(v[0], 3, 1)
        for c in range(1, count):
            packed = jnp.where(lane >= 8 * c, pltpu.roll(v[c], 8 * c + 3, 1), packed)
        return packed

    for q in range(12):
        send_ref[16 * q : 16 * q + 16, :] = some(16 * q, 16)
    send_ref[192:208, :] = some(192, 8)
    wide = lax.broadcasted_iota(jnp.int32, (C, LANES), 1)

    def edge(first):
        rows = [o_ref[pl.ds(first + k, C, stride=ROWS), :] for k in range(3)]
        corner = pltpu.roll(rows[0], 3, 1)
        for k in range(1, 3):
            corner = jnp.where(wide >= 8 * k, pltpu.roll(rows[k], 8 * k + 3, 1), corner)
        return rows, pack_corner(corner)

    fill = jnp.zeros((8, LANES), F32)
    low, low_corner = edge(0)
    bot_ref[...] = jnp.concatenate(low + [fill], axis=0).astype(BF16)
    high, high_corner = edge(ROWS - 3)
    send_ref[PAD:, :] = jnp.concatenate(high + [low_corner, high_corner, fill], axis=0).astype(BF16)


EDGE_SHAPES = (
    jax.ShapeDtypeStruct((SEND, LANES), BF16),
    jax.ShapeDtypeStruct((BOT, LANES), BF16),
)


def first_kernel(x_ref, send_ref, bot_ref, o_ref):
    emit_edges(lambda first, count: x_ref[pl.ds(first, count)].astype(F32), o_ref, None, send_ref, bot_ref)


def first_edges(x):
    return pl.pallas_call(
        first_kernel,
        out_shape=EDGE_SHAPES,
        in_specs=[VM],
        out_specs=(VM,) * 2,
        scratch_shapes=[pltpu.VMEM((C * ROWS, LANES), F32)],
        compiler_params=pltpu.CompilerParams(vmem_limit_bytes=6 * 2**20),
    )(x)


def place_on_mesh():
    level = lax.axis_index("merid")
    return level == lax.axis_size("merid") - 1, level % 2


def turn_kernel(fold_ref, west_ref, east_ref, send_ref, bot_ref, q1_ref, q2_ref, up_ref):
    at_top, odd = place_on_mesh()
    off = (fold_ref[0] + (LANES // 2 + 1)) % LANES - LANES // 2
    lane = lax.broadcasted_iota(jnp.int32, (PACK, LANES), 1)
    parts = [ref[PAD:, :] for ref in (west_ref, send_ref, east_ref)]
    wide = [part.astype(F32) for part in parts]

    def corner(at):
        return jnp.where((lane & 7) < 3, wide[0][at : at + PACK], wide[2][at : at + PACK])

    @pl.when(jnp.logical_not(at_top))
    def _():
        up = jnp.concatenate([wide[1][: 3 * C], corner(3 * C + PACK)], axis=0)
        up_ref[...] = up.astype(BF16)

    @pl.when(at_top)
    def _():
        src = lax.broadcasted_iota(jnp.int32, (LANES, 2 * LANES), 0)
        dst = lax.broadcasted_iota(jnp.int32, (LANES, 2 * LANES), 1)
        col = jnp.where(dst < LANES, dst, jnp.where(dst < LANES + 3, dst - LANES - 3, dst - 3))
        used = dst < LANES + 6
        turned = jnp.zeros((SEND - PAD, 2 * LANES), F32)
        for n in range(3):
            hit = used & (src + 128 * (n - 1) + col == off + 127)
            turned += dot32(parts[n], jnp.where(hit, 1.0, 0.0).astype(BF16))
        rows = [turned[(2 - k) * C : (3 - k) * C, :LANES] for k in range(3)]
        ends = [turned[(2 - k) * C : (3 - k) * C, LANES:] for k in range(3)]
        full_lane = lax.broadcasted_iota(jnp.int32, (C, LANES), 1)
        turned_corner = ends[0]
        for k in range(1, 3):
            turned_corner = jnp.where(full_lane >= 8 * k, pltpu.roll(ends[k], 8 * k, 1), turned_corner)
        up_ref[...] = jnp.concatenate(rows + [pack_corner(turned_corner)], axis=0).astype(BF16)

    def put(to_up_ref, to_down_ref):
        to_up_ref[...] = up_ref[...]
        down = jnp.concatenate([bot_ref[...].astype(F32)[: 3 * C], corner(3 * C)], axis=0)
        to_down_ref[...] = down.astype(BF16)

    pl.when(odd == 0)(lambda: put(q1_ref, q2_ref))
    pl.when(odd == 1)(lambda: put(q2_ref, q1_ref))


def turn_edges(fold, west, east, send, bot):
    return pl.pallas_call(
        turn_kernel,
        out_shape=(jax.ShapeDtypeStruct((SWAP, LANES), BF16),) * 2,
        in_specs=[SM] + [VM] * 4,
        out_specs=(VM, VM),
        scratch_shapes=[pltpu.VMEM((SWAP, LANES), BF16)],
        compiler_params=pltpu.CompilerParams(vmem_limit_bytes=6 * 2**20),
    )(fold, west, east, send, bot)


def shifted(full, ends, lane, e):
    s = e - 3
    if s > 0:
        return pltpu.roll(jnp.where(lane < s, ends, full), LANES - s, 1)
    if s < 0:
        return pltpu.roll(jnp.where(lane >= LANES + s, ends, full), -s, 1)
    return full


UNROLL = 5


def conv_kernel(x_ref, band_ref, west_ref, east_ref, y_far, side_ref, y_ref, sem):
    lane = lanes_bf16(MAIN)
    tile_lane = lax.broadcasted_iota(jnp.int32, (ROWS, LANES), 1)
    for q in range(13):
        both = jnp.where(
            (tile_lane & 7) < 3,
            west_ref[16 * q : 16 * q + 16, :].astype(F32),
            east_ref[16 * q : 16 * q + 16, :].astype(F32),
        ).astype(BF16)
        for c in range(16 if q < 12 else 8):
            side_ref[16 * q + c] = pltpu.roll(both, LANES - (8 * c + 3), 1)

    def some(t, carry):
        for u in range(UNROLL):
            g = UNROLL * t + u
            full = x_ref[pl.ds(8 * g, 8)].reshape(MAIN, LANES)
            ends = side_ref[pl.ds(8 * g, 8)].reshape(MAIN, LANES)
            rhs = jnp.concatenate([shifted(full, ends, lane, e) for e in range(7)], axis=0)
            y_ref[:, g] = dot32(band_ref[g], rhs).reshape(ROWS, 8, LANES)
        part = pl.ds(UNROLL * t, UNROLL)
        pltpu.make_async_copy(y_ref.at[:, part], y_far.at[:, part], sem).start()
        return carry

    lax.fori_loop(0, GROUPS // UNROLL, some, 0)
    pltpu.make_async_copy(y_ref, y_far, sem).wait()


def conv_own(x, band, west, east):
    return pl.pallas_call(
        conv_kernel,
        out_shape=jax.ShapeDtypeStruct((ROWS, GROUPS, 8, LANES), F32),
        in_specs=[VM] * 4,
        out_specs=ANY,
        scratch_shapes=[
            pltpu.VMEM((C, ROWS, LANES), BF16),
            pltpu.VMEM((ROWS, GROUPS, 8, LANES), F32),
            pltpu.SemaphoreType.DMA(()),
        ],
        compiler_params=pltpu.CompilerParams(vmem_limit_bytes=14 * 2**20),
        cost_estimate=pl.CostEstimate(flops=2 * 25 * 256 * 256 * 1024, bytes_accessed=9_000_000, transcendentals=0),
    )(x, band, west, east)


def gelu(h):
    return h * (0.5 + 0.5 * lax.erf(h * np.float32(0.5**0.5)))


def block_kernel(last, block, x_ref, y_far, band_ref, r1_ref, r2_ref, r3_ref, w1_ref, w2_ref, gain_ref, mask_ref,
                 out_ref, *refs):
    edge_refs, (r32_ref, c32_ref, add_ref, o_ref, y_ref, sem) = refs[:-6], refs[-6:]
    fetch = pltpu.make_async_copy(y_far, y_ref, sem)
    fetch.start()
    at_top, odd = place_on_mesh()

    def put(below_ref, above_ref):
        for base, ref in ((0, below_ref), (3, above_ref)):
            v = ref[...].astype(F32)
            for k in range(3):
                r32_ref[base + k] = v[k * C : (k + 1) * C].reshape(GROUPS, 8, LANES)
                for q in range(C // PACK):
                    corner = pltpu.roll(v[3 * C :], LANES - (24 * q + 8 * k + 3), 1)
                    c32_ref[base + k, 5 * q : 5 * q + 5] = corner.reshape(5, 8, LANES)

    pl.when(odd == 0)(lambda: put(r2_ref, r1_ref))
    pl.when((odd == 1) & jnp.logical_not(at_top))(lambda: put(r1_ref, r2_ref))
    pl.when(at_top)(lambda: put(r1_ref, r3_ref))
    lane = lanes_bf16(SIDE)

    def halo(g, carry):
        full = r32_ref[:, g].reshape(SIDE, LANES).astype(BF16)
        ends = c32_ref[:, g].reshape(SIDE, LANES).astype(BF16)
        rhs = jnp.concatenate([shifted(full, ends, lane, e) for e in range(7)], axis=0)
        add_ref[:, g] = dot32(band_ref[g], rhs).reshape(6, 8, LANES)
        return carry

    lax.fori_loop(0, GROUPS, halo, 0, unroll=25)

    fetch.wait()

    def mlp(i0, edges):
        parts = []
        for r in range(2):
            y = y_ref[i0 + r].reshape(C, LANES)
            if edges[r] is not None:
                y = y + add_ref[edges[r]].reshape(C, LANES)
            mean = jnp.sum(y, axis=0, keepdims=True) * np.float32(1 / C)
            y = y - mean
            var = jnp.sum(y * y, axis=0, keepdims=True) * np.float32(1 / C)
            parts.append((y * lax.rsqrt(var + EPS) * gain_ref[...]).astype(BF16))
        hidden = gelu(dot32(w1_ref[...], jnp.concatenate(parts, axis=1))).astype(BF16)
        o = dot32(w2_ref[block], hidden)
        for r in range(2):
            o_ref[pl.ds(i0 + r, C, stride=ROWS), :] = o[:, r * LANES : (r + 1) * LANES]

    edge_of = {row: n for n, row in enumerate(EDGE_ROWS)}
    for i in range(0, ROWS, 2):
        mlp(i, (edge_of.get(i), edge_of.get(i + 1)))
    mask = mask_ref[...]

    def tile(first, count):
        o = o_ref[pl.ds(first * ROWS, count * ROWS), :].reshape(count, ROWS, LANES)
        return (x_ref[pl.ds(first, count)].astype(F32) + o) * mask[None]

    if last:
        def finish(g, carry):
            out_ref[pl.ds(8 * g, 8)] = tile(pl.multiple_of(8 * g, 8), 8).astype(BF16)
            return carry

        lax.fori_loop(0, GROUPS, finish, 0)
    else:
        emit_edges(tile, o_ref, out_ref, *edge_refs)


def run_block(last, block, x, y, band, r1, r2, r3, w1, w2, gain, mask):
    state = jax.ShapeDtypeStruct((C, ROWS, LANES), BF16)
    shapes = (state,) if last else (state,) + EDGE_SHAPES
    return pl.pallas_call(
        lambda *refs: block_kernel(last, block, *refs),
        out_shape=shapes,
        in_specs=[VM, ANY] + [VM] * 8,
        out_specs=(VM,) * len(shapes),
        scratch_shapes=[
            pltpu.VMEM((6, GROUPS, 8, LANES), F32),
            pltpu.VMEM((6, GROUPS, 8, LANES), F32),
            pltpu.VMEM((6, GROUPS, 8, LANES), F32),
            pltpu.VMEM((C * ROWS, LANES), F32),
            pltpu.VMEM((ROWS, GROUPS, 8, LANES), F32),
            pltpu.SemaphoreType.DMA(()),
        ],
        compiler_params=pltpu.CompilerParams(vmem_limit_bytes=16 * 2**20),
    )(x, y, band, r1, r2, r3, w1, w2, gain, mask)


def local(field, land_mask, fold_partner, dw_kernel, norm_gain, w_in, w_out):
    zonal = lax.axis_size("zonal")
    merid = lax.axis_size("merid")
    total = fold_partner.shape[0]
    start = jnp.mod(fold_partner[0] - (LANES // 2 - 1), total)
    turn = start // LANES
    place = lambda m, z: z * merid + m
    even_pairs = [(m, m ^ 1) for m in range(merid)]
    odd_pairs = [(m, ((m - 1) ^ 1) + 1) for m in range(1, merid - 1)]

    def branch_of(shift):
        def branch(rows, mask, *kept):
            pairs = [(place(merid - 1, z), place(merid - 1, (shift - z) % zonal)) for z in range(zonal)]
            return lax.ppermute(rows, ("zonal", "merid"), pairs), float_mask(mask, *kept)

        return branch

    branches = [branch_of(t) for t in range(zonal)]
    taps = jnp.transpose(dw_kernel, (0, 2, 3, 1))
    w2 = jnp.swapaxes(w_out, 1, 2)
    x = field
    send, bot = first_edges(x)
    for b in range(BLOCKS):
        west = lax.ppermute(send, "zonal", [(z, (z + 1) % zonal) for z in range(zonal)])
        east = lax.ppermute(send, "zonal", [((z + 1) % zonal, z) for z in range(zonal)])
        band_main, band_side, w1, gain = make_bands(b, taps, w_in, norm_gain)
        q1, q2 = turn_edges(fold_partner, west, east, send, bot)
        r1 = lax.ppermute(q1, "merid", even_pairs)
        r2 = lax.ppermute(q2, "merid", odd_pairs)
        y = conv_own(x, band_main, west, east)
        q2, y = lax.optimization_barrier((q2, y))
        r3, mask = lax.switch(turn, branches, q2, land_mask, x, y, band_side, w1, gain)
        last = b == BLOCKS - 1
        x, *edges = run_block(last, b, x, y, band_side, r1, r2, r3, w1, w2, gain, mask)
        if not last:
            send, bot = edges
    return x


def mask_kernel(mask_ref, *refs):
    out_ref = refs[-1]
    out_ref[...] = mask_ref[...].astype(F32)


def float_mask(mask, *kept):
    return pl.pallas_call(
        mask_kernel,
        out_shape=jax.ShapeDtypeStruct((ROWS, LANES), F32),
        in_specs=[VM] + [pl.BlockSpec(memory_space=pl.ANY)] * len(kept),
        out_specs=VM,
        compiler_params=pltpu.CompilerParams(vmem_limit_bytes=4 * 2**20),
    )(mask, *kept)


def solution(mesh):
    in_specs = (P(None, "merid", "zonal"), P("merid", "zonal"), P(), P(), P(), P(), P())
    out_specs = P(None, "merid", "zonal")
    return jax.shard_map(local, mesh=mesh, in_specs=in_specs, out_specs=out_specs, check_vma=False)
```

profile of v0, /device:TPU:6, one launch (start us, length us, event | category | flops | bytes accessed | tf_op | source)
XLA Modules:
  0.0 97.7 jit_solution(13481942995447089747)
XLA Ops:
  0.0 1.7 %shard_map.73 = (bf16[896,128]{1,0:T(8,128)(2,1)S(1)}, bf16[608,128]{1,0:T(8,128)(2,1)S(1)}) custom-call(bf16[200,16,128]{2,1,0:T(8,128)(2,1)} %refs_0_.1), custom_call_target="tpu_custom_call" | custom-call | tf_op jit(solution)/shard_map/pallas_call | solution.py:156
  1.8 3.9 %collective-permute-start.49 = (bf16[896,128]{1,0:T(8,128)(2,1)S(1)}, bf16[896,128]{1,0:T(8,128)(2,1)S(1)}, u32[]{:S(2)}, u32[]{:S(2)}) collective-permute-start(bf16[896,128]{1,0:T(8,128)(2,1)S(1)} %get-tuple-element.1051.send_ref), channel_id=1, source_target_pairs={{8,0},{16,8},{24,16},{32,24},{40,32},{48,40},{56,48},{64,56},{72,6... | collective-permute-start | bytes 688136 | tf_op jit(solution)/shard_map/ppermute | solution.py:393
  7.6 1.2 %copy-done.2 = bf16[3,200,800]{2,1,0:T(8,128)(2,1)S(1)} copy-done((bf16[3,200,800]{2,1,0:T(8,128)(2,1)S(1)}, bf16[3,200,800]{2,1,0:T(8,128)(2,1)}, u32[]{:S(2)}) %copy-start.2) | copy-done | bytes 960024
  10.4 2.7 %shard_map.75 = (bf16[25,128,896]{2,1,0:T(8,128)(2,1)S(1)}, bf16[25,48,336]{2,1,0:T(8,128)(2,1)S(1)}, bf16[800,200]{1,0:T(8,128)(2,1)S(1)}, f32[200,128]{1,0:T(8,128)S(1)}) custom-call(bf16[3,7,7,200]{3,2,1,0:T(8,128)(2,1)S(1)} %bitcast.6, bf16[3,200,800]{2,1,0:T(8,128)(2,1)S(1)} %copy-done.2, bf16[3,200]{1,0:T(4,128)(2,1)S(1)} %copy-done.6), custom_call_target="tpu_custom_call" | custom-call | flops 2147483648 | bytes 9000000 | tf_op jit(solution)/shard_map/pallas_call | solution.py:97
  13.2 1.5 %shard_map.74 = (bf16[640,128]{1,0:T(8,128)(2,1)S(1)}, bf16[640,128]{1,0:T(8,128)(2,1)}) custom-call(s32[2048]{0:T(1024)S(1)} %copy-done.1, bf16[896,128]{1,0:T(8,128)(2,1)S(1)} %collective-permute-done.48.west_ref, bf16[896,128]{1,0:T(8,128)(2,1)S(1)} %collective-permute-done.49.east_ref, bf16[896,128]{1,0:T(8,128)(2,1)S(1)} %get-tuple-element.1051.send_ref, ...), custom_call_target="tpu_custom_call" | custom-call | tf_op jit(solution)/shard_map/pallas_call | solution.py:214
  14.6 4.3 %collective-permute-start.50 = (bf16[640,128]{1,0:T(8,128)(2,1)S(1)}, bf16[640,128]{1,0:T(8,128)(2,1)S(1)}, u32[]{:S(2)}, u32[]{:S(2)}) collective-permute-start(bf16[640,128]{1,0:T(8,128)(2,1)S(1)} %get-tuple-element.1057), channel_id=1, source_target_pairs={{0,1},{1,0},{2,3},{3,2},{4,5},{5,4},{6,7},{7,6},{8,9},{9,8},{10,11... | collective-permute-start | bytes 491528 | tf_op jit(solution)/shard_map/ppermute | solution.py:396
  19.0 1.9 %collective-permute-start.51 = (bf16[640,128]{1,0:T(8,128)(2,1)}, bf16[640,128]{1,0:T(8,128)(2,1)S(1)}, u32[]{:S(2)}, u32[]{:S(2)}) collective-permute-start(bf16[640,128]{1,0:T(8,128)(2,1)} %get-tuple-element.1058), channel_id=1, source_target_pairs={{1,2},{2,1},{3,4},{4,3},{5,6},{6,5},{9,10},{10,9},{11,12},{12,11},... | collective-permute-start | bytes 491528 | tf_op jit(solution)/shard_map/ppermute | solution.py:397
  20.9 3.7 %shard_map.76.refs_1_ = f32[16,25,8,128]{3,2,1,0:T(8,128)} custom-call(bf16[200,16,128]{2,1,0:T(8,128)(2,1)S(1)} %copy-done.10, bf16[25,128,896]{2,1,0:T(8,128)(2,1)S(1)} %get-tuple-element.1054.band_ref, bf16[896,128]{1,0:T(8,128)(2,1)S(1)} %collective-permute-done.48.west_ref, bf16[896,128]{1,0:T(8,128)(2,1)S(1)} %collective-permute-done.49.east_ref), custom_call_target="tpu_custom_call" | custom-call | flops 3355443200 | bytes 9000000 | tf_op jit(solution)/shard_map/pallas_call | solution.py:264
  24.6 1.5 %conditional.3 = (bf16[640,128]{1,0:T(8,128)(2,1)}, f32[16,128]{1,0:T(8,128)S(1)}) conditional(s32[]{:T(128)} %clamp.2, (bf16[640,128]{1,0:T(8,128)(2,1)}, s32[16,128]{1,0:T(8,128)S(1)}, bf16[200,16,128]{2,1,0:T(8,128)(2,1)S(1)}, f32[16,25,8,128]{3,2,1,0:T(8,128)}, bf16[25,48,336]{2,1,0:T(8,128)(2,1)S(1)}, ...), branch_computations={%region_0.1_spmd, %region_1.2_spmd, %region_2.3_spmd, %region_3.4_... | conditional | bytes 655416 | solution.py:400
  24.7 1.5 %collective-permute-start.15 = (bf16[640,128]{1,0:T(8,128)(2,1)}, bf16[640,128]{1,0:T(8,128)(2,1)}, u32[]{:S(2)}, u32[]{:S(2)}) collective-permute-start(bf16[640,128]{1,0:T(8,128)(2,1)} %get-tuple-element.782), channel_id=1, source_target_pairs={{7,127},{15,119},{23,111},{31,103},{39,95},{47,87},{55,79},{63,71}... | collective-permute-start | bytes 491528 | tf_op jit(solution)/shard_map/cond/branch_15_fun/ppermute | solution.py:382
  26.2 3.0 %collective-permute-done.51.refs_4_ = bf16[640,128]{1,0:T(8,128)(2,1)S(1)} collective-permute-done((bf16[640,128]{1,0:T(8,128)(2,1)}, bf16[640,128]{1,0:T(8,128)(2,1)S(1)}, u32[]{:S(2)}, u32[]{:S(2)}) %collective-permute-start.51) | collective-permute-done | bytes 163872 | tf_op jit(solution)/shard_map/ppermute | solution.py:397
  29.2 6.4 %shard_map.77 = (bf16[200,16,128]{2,1,0:T(8,128)(2,1)S(1)}, bf16[896,128]{1,0:T(8,128)(2,1)S(1)}, bf16[608,128]{1,0:T(8,128)(2,1)S(1)}) custom-call(bf16[200,16,128]{2,1,0:T(8,128)(2,1)} %refs_0_.1, f32[16,25,8,128]{3,2,1,0:T(8,128)} %shard_map.76.refs_1_, bf16[25,48,336]{2,1,0:T(8,128)(2,1)S(1)} %get-tuple-element.1056.refs_2_, ...), custom_call_target="tpu_custom_call" | custom-call | tf_op jit(solution)/shard_map/pallas_call | solution.py:352
  35.7 3.8 %collective-permute-start.53 = (bf16[896,128]{1,0:T(8,128)(2,1)S(1)}, bf16[896,128]{1,0:T(8,128)(2,1)S(1)}, u32[]{:S(2)}, u32[]{:S(2)}) collective-permute-start(bf16[896,128]{1,0:T(8,128)(2,1)S(1)} %get-tuple-element.1064.send_ref), channel_id=1, source_target_pairs={{8,0},{16,8},{24,16},{32,24},{40,32},{48,40},{56,48},{64,56},{72,6... | collective-permute-start | bytes 688136 | tf_op jit(solution)/shard_map/ppermute | solution.py:393
  39.5 2.7 %shard_map.79 = (bf16[25,128,896]{2,1,0:T(8,128)(2,1)S(1)}, bf16[25,48,336]{2,1,0:T(8,128)(2,1)S(1)}, bf16[800,200]{1,0:T(8,128)(2,1)S(1)}, f32[200,128]{1,0:T(8,128)S(1)}) custom-call(bf16[3,7,7,200]{3,2,1,0:T(8,128)(2,1)S(1)} %bitcast.7, bf16[3,200,800]{2,1,0:T(8,128)(2,1)S(1)} %copy-done.3, bf16[3,200]{1,0:T(4,128)(2,1)S(1)} %copy-done.7), custom_call_target="tpu_custom_call" | custom-call | flops 2147483648 | bytes 9000000 | tf_op jit(solution)/shard_map/pallas_call | solution.py:97
  43.2 1.5 %shard_map.78 = (bf16[640,128]{1,0:T(8,128)(2,1)S(1)}, bf16[640,128]{1,0:T(8,128)(2,1)}) custom-call(s32[2048]{0:T(1024)S(1)} %copy-done.1, bf16[896,128]{1,0:T(8,128)(2,1)S(1)} %collective-permute-done.52.west_ref, bf16[896,128]{1,0:T(8,128)(2,1)S(1)} %collective-permute-done.53.east_ref, bf16[896,128]{1,0:T(8,128)(2,1)S(1)} %get-tuple-element.1064.send_ref, ...), custom_call_target="tpu_custom_call" | custom-call | tf_op jit(solution)/shard_map/pallas_call | solution.py:214
  44.7 5.4 %collective-permute-start.54 = (bf16[640,128]{1,0:T(8,128)(2,1)S(1)}, bf16[640,128]{1,0:T(8,128)(2,1)S(1)}, u32[]{:S(2)}, u32[]{:S(2)}) collective-permute-start(bf16[640,128]{1,0:T(8,128)(2,1)S(1)} %get-tuple-element.1070), channel_id=1, source_target_pairs={{0,1},{1,0},{2,3},{3,2},{4,5},{5,4},{6,7},{7,6},{8,9},{9,8},{10,11... | collective-permute-start | bytes 491528 | tf_op jit(solution)/shard_map/ppermute | solution.py:396
  50.0 1.9 %collective-permute-start.55 = (bf16[640,128]{1,0:T(8,128)(2,1)}, bf16[640,128]{1,0:T(8,128)(2,1)S(1)}, u32[]{:S(2)}, u32[]{:S(2)}) collective-permute-start(bf16[640,128]{1,0:T(8,128)(2,1)} %get-tuple-element.1071), channel_id=1, source_target_pairs={{1,2},{2,1},{3,4},{4,3},{5,6},{6,5},{9,10},{10,9},{11,12},{12,11},... | collective-permute-start | bytes 491528 | tf_op jit(solution)/shard_map/ppermute | solution.py:397
  51.9 3.6 %shard_map.80.refs_1_ = f32[16,25,8,128]{3,2,1,0:T(8,128)} custom-call(bf16[200,16,128]{2,1,0:T(8,128)(2,1)S(1)} %get-tuple-element.1063.x_ref.refs_0_, bf16[25,128,896]{2,1,0:T(8,128)(2,1)S(1)} %get-tuple-element.1067.band_ref, bf16[896,128]{1,0:T(8,128)(2,1)S(1)} %collective-permute-done.52.west_ref, bf16[896,128]{1,0:T(8,128)(2,1)S(1)} %collective-permute-done.53.east_ref), custom_call_target="tpu_custom_call" | custom-call | flops 3355443200 | bytes 9000000 | tf_op jit(solution)/shard_map/pallas_call | solution.py:264
  55.6 1.4 %conditional.4 = (bf16[640,128]{1,0:T(8,128)(2,1)}, f32[16,128]{1,0:T(8,128)S(1)}) conditional(s32[]{:T(128)} %clamp.2, (bf16[640,128]{1,0:T(8,128)(2,1)}, s32[16,128]{1,0:T(8,128)S(1)}, bf16[200,16,128]{2,1,0:T(8,128)(2,1)S(1)}, f32[16,25,8,128]{3,2,1,0:T(8,128)}, bf16[25,48,336]{2,1,0:T(8,128)(2,1)S(1)}, ...), branch_computations={%region_16.17_spmd, %region_17.18_spmd, %region_18.19_spmd, %regio... | conditional | bytes 655416 | solution.py:400
  55.7 1.3 %collective-permute-start.31 = (bf16[640,128]{1,0:T(8,128)(2,1)}, bf16[640,128]{1,0:T(8,128)(2,1)}, u32[]{:S(2)}, u32[]{:S(2)}) collective-permute-start(bf16[640,128]{1,0:T(8,128)(2,1)} %get-tuple-element.894), channel_id=1, source_target_pairs={{7,127},{15,119},{23,111},{31,103},{39,95},{47,87},{55,79},{63,71}... | collective-permute-start | bytes 491528 | tf_op jit(solution)/shard_map/cond/branch_15_fun/ppermute | solution.py:382
  57.0 4.6 %collective-permute-done.55.refs_4_ = bf16[640,128]{1,0:T(8,128)(2,1)S(1)} collective-permute-done((bf16[640,128]{1,0:T(8,128)(2,1)}, bf16[640,128]{1,0:T(8,128)(2,1)S(1)}, u32[]{:S(2)}, u32[]{:S(2)}) %collective-permute-start.55) | collective-permute-done | bytes 163872 | tf_op jit(solution)/shard_map/ppermute | solution.py:397
  61.6 6.5 %shard_map.81 = (bf16[200,16,128]{2,1,0:T(8,128)(2,1)S(1)}, bf16[896,128]{1,0:T(8,128)(2,1)S(1)}, bf16[608,128]{1,0:T(8,128)(2,1)S(1)}) custom-call(bf16[200,16,128]{2,1,0:T(8,128)(2,1)} %copy-done.11, f32[16,25,8,128]{3,2,1,0:T(8,128)} %shard_map.80.refs_1_, bf16[25,48,336]{2,1,0:T(8,128)(2,1)} %copy-done.8, ...), custom_call_target="tpu_custom_call" | custom-call | tf_op jit(solution)/shard_map/pallas_call | solution.py:352
  68.2 3.8 %collective-permute-start.57 = (bf16[896,128]{1,0:T(8,128)(2,1)S(1)}, bf16[896,128]{1,0:T(8,128)(2,1)S(1)}, u32[]{:S(2)}, u32[]{:S(2)}) collective-permute-start(bf16[896,128]{1,0:T(8,128)(2,1)S(1)} %get-tuple-element.1077.send_ref), channel_id=1, source_target_pairs={{8,0},{16,8},{24,16},{32,24},{40,32},{48,40},{56,48},{64,56},{72,6... | collective-permute-start | bytes 688136 | tf_op jit(solution)/shard_map/ppermute | solution.py:393
  72.0 2.7 %shard_map.83 = (bf16[25,128,896]{2,1,0:T(8,128)(2,1)S(1)}, bf16[25,48,336]{2,1,0:T(8,128)(2,1)S(1)}, bf16[800,200]{1,0:T(8,128)(2,1)S(1)}, f32[200,128]{1,0:T(8,128)S(1)}) custom-call(bf16[3,7,7,200]{3,2,1,0:T(8,128)(2,1)S(1)} %bitcast.8, bf16[3,200,800]{2,1,0:T(8,128)(2,1)S(1)} %copy-done.3, bf16[3,200]{1,0:T(4,128)(2,1)S(1)} %copy-done.7), custom_call_target="tpu_custom_call" | custom-call | flops 2147483648 | bytes 9000000 | tf_op jit(solution)/shard_map/pallas_call | solution.py:97
  75.7 1.7 %shard_map.82 = (bf16[640,128]{1,0:T(8,128)(2,1)S(1)}, bf16[640,128]{1,0:T(8,128)(2,1)}) custom-call(s32[2048]{0:T(1024)S(1)} %copy-done.1, bf16[896,128]{1,0:T(8,128)(2,1)S(1)} %collective-permute-done.56.west_ref, bf16[896,128]{1,0:T(8,128)(2,1)S(1)} %collective-permute-done.57.east_ref, bf16[896,128]{1,0:T(8,128)(2,1)S(1)} %get-tuple-element.1077.send_ref, ...), custom_call_target="tpu_custom_call" | custom-call | tf_op jit(solution)/shard_map/pallas_call | solution.py:214
  77.4 2.8 %collective-permute-start.58 = (bf16[640,128]{1,0:T(8,128)(2,1)S(1)}, bf16[640,128]{1,0:T(8,128)(2,1)S(1)}, u32[]{:S(2)}, u32[]{:S(2)}) collective-permute-start(bf16[640,128]{1,0:T(8,128)(2,1)S(1)} %get-tuple-element.1083), channel_id=1, source_target_pairs={{0,1},{1,0},{2,3},{3,2},{4,5},{5,4},{6,7},{7,6},{8,9},{9,8},{10,11... | collective-permute-start | bytes 491528 | tf_op jit(solution)/shard_map/ppermute | solution.py:396
  80.2 1.9 %collective-permute-start.59 = (bf16[640,128]{1,0:T(8,128)(2,1)}, bf16[640,128]{1,0:T(8,128)(2,1)S(1)}, u32[]{:S(2)}, u32[]{:S(2)}) collective-permute-start(bf16[640,128]{1,0:T(8,128)(2,1)} %get-tuple-element.1084), channel_id=1, source_target_pairs={{1,2},{2,1},{3,4},{4,3},{5,6},{6,5},{9,10},{10,9},{11,12},{12,11},... | collective-permute-start | bytes 491528 | tf_op jit(solution)/shard_map/ppermute | solution.py:397
  82.1 3.0 %shard_map.84.refs_1_ = f32[16,25,8,128]{3,2,1,0:T(8,128)S(1)} custom-call(bf16[200,16,128]{2,1,0:T(8,128)(2,1)S(1)} %get-tuple-element.1076.x_ref.refs_0_, bf16[25,128,896]{2,1,0:T(8,128)(2,1)S(1)} %get-tuple-element.1080.band_ref, bf16[896,128]{1,0:T(8,128)(2,1)S(1)} %collective-permute-done.56.west_ref, bf16[896,128]{1,0:T(8,128)(2,1)S(1)} %collective-permute-done.57.east_ref), custom_call_target="tpu_custom_call" | custom-call | flops 3355443200 | bytes 9000000 | tf_op jit(solution)/shard_map/pallas_call | solution.py:264
  85.1 1.4 %conditional.5 = (bf16[640,128]{1,0:T(8,128)(2,1)}, f32[16,128]{1,0:T(8,128)S(1)}) conditional(s32[]{:T(128)} %clamp.2, (bf16[640,128]{1,0:T(8,128)(2,1)}, s32[16,128]{1,0:T(8,128)S(1)}, bf16[200,16,128]{2,1,0:T(8,128)(2,1)S(1)}, f32[16,25,8,128]{3,2,1,0:T(8,128)S(1)}, bf16[25,48,336]{2,1,0:T(8,128)(2,1)S(1)}, ...), branch_computations={%region_32.33_spmd, %region_33.34_spmd, %region_34.35_spmd, %regio... | conditional | bytes 655416 | solution.py:400
  85.2 1.3 %collective-permute-start.47 = (bf16[640,128]{1,0:T(8,128)(2,1)}, bf16[640,128]{1,0:T(8,128)(2,1)}, u32[]{:S(2)}, u32[]{:S(2)}) collective-permute-start(bf16[640,128]{1,0:T(8,128)(2,1)} %get-tuple-element.1006), channel_id=1, source_target_pairs={{7,127},{15,119},{23,111},{31,103},{39,95},{47,87},{55,79},{63,71}... | collective-permute-start | bytes 491528 | tf_op jit(solution)/shard_map/cond/branch_15_fun/ppermute | solution.py:382
  86.6 4.4 %collective-permute-done.59.refs_4_ = bf16[640,128]{1,0:T(8,128)(2,1)S(1)} collective-permute-done((bf16[640,128]{1,0:T(8,128)(2,1)}, bf16[640,128]{1,0:T(8,128)(2,1)S(1)}, u32[]{:S(2)}, u32[]{:S(2)}) %collective-permute-start.59) | collective-permute-done | bytes 163872 | tf_op jit(solution)/shard_map/ppermute | solution.py:397
  91.0 6.6 %shard_map.85 = bf16[200,16,128]{2,1,0:T(8,128)(2,1)} custom-call(bf16[200,16,128]{2,1,0:T(8,128)(2,1)} %copy-done.12, f32[16,25,8,128]{3,2,1,0:T(8,128)S(1)} %shard_map.84.refs_1_, bf16[25,48,336]{2,1,0:T(8,128)(2,1)} %copy-done.9, bf16[640,128]{1,0:T(8,128)(2,1)S(1)} %collective-permute-done.58.refs_3_, ...), custom_call_target="tpu_custom_call" | custom-call | tf_op jit(solution)/shard_map/pallas_call | solution.py:352
  (52 shorter events, 5.0 us)
Async XLA Ops:
  1.7 11.4 %collective-permute-start.48 = (bf16[896,128]{1,0:T(8,128)(2,1)S(1)}, bf16[896,128]{1,0:T(8,128)(2,1)S(1)}, u32[]{:S(2)}, u32[]{:S(2)}) collective-permute-start(bf16[896,128]{1,0:T(8,128)(2,1)S(1)} %get-tuple-element.1051.send_ref), channel_id=1, source_target_pairs={{0,8},{8,16},{16,24},{24,32},{32,40},{40,48},{48,56},{56,64},{64,7... | collective-permute-start | bytes 688136 | tf_op jit(solution)/shard_map/ppermute | solution.py:392
  1.8 11.3 %collective-permute-start.49 = (bf16[896,128]{1,0:T(8,128)(2,1)S(1)}, bf16[896,128]{1,0:T(8,128)(2,1)S(1)}, u32[]{:S(2)}, u32[]{:S(2)}) collective-permute-start(bf16[896,128]{1,0:T(8,128)(2,1)S(1)} %get-tuple-element.1051.send_ref), channel_id=1, source_target_pairs={{8,0},{16,8},{24,16},{32,24},{40,32},{48,40},{56,48},{64,56},{72,6... | collective-permute-start | bytes 688136 | tf_op jit(solution)/shard_map/ppermute | solution.py:393
  7.6 1.2 %copy-start.2 = (bf16[3,200,800]{2,1,0:T(8,128)(2,1)S(1)}, bf16[3,200,800]{2,1,0:T(8,128)(2,1)}, u32[]{:S(2)}) copy-start(bf16[3,200,800]{2,1,0:T(8,128)(2,1)} %refs_1_.5) | copy-start | bytes 2880004
  8.8 0.9 copy-start.4
  9.7 0.7 copy-start.6
  10.4 2.8 %copy-start.1 = (s32[2048]{0:T(1024)S(1)}, s32[2048]{0:T(1024)}, u32[]{:S(2)}) copy-start(s32[2048]{0:T(1024)} %fold_ref.5) | copy-start | bytes 24580
  10.4 10.5 %copy-start.10 = (bf16[200,16,128]{2,1,0:T(8,128)(2,1)S(1)}, bf16[200,16,128]{2,1,0:T(8,128)(2,1)}, u32[]{:S(2)}) copy-start(bf16[200,16,128]{2,1,0:T(8,128)(2,1)} %refs_0_.1) | copy-start | bytes 2457604
  13.1 11.5 %copy-start.13 = (bf16[800,200]{1,0:T(8,128)(2,1)}, bf16[800,200]{1,0:T(8,128)(2,1)S(1)}, u32[]{:S(2)}) copy-start(bf16[800,200]{1,0:T(8,128)(2,1)S(1)} %get-tuple-element.1059.refs_6_) | copy-start | bytes 960004
  13.1 11.5 %copy-start.15 = (f32[200,128]{1,0:T(8,128)}, f32[200,128]{1,0:T(8,128)S(1)}, u32[]{:S(2)}) copy-start(f32[200,128]{1,0:T(8,128)S(1)} %get-tuple-element.1060.refs_8_) | copy-start | bytes 307204
  14.6 11.5 %collective-permute-start.50 = (bf16[640,128]{1,0:T(8,128)(2,1)S(1)}, bf16[640,128]{1,0:T(8,128)(2,1)S(1)}, u32[]{:S(2)}, u32[]{:S(2)}) collective-permute-start(bf16[640,128]{1,0:T(8,128)(2,1)S(1)} %get-tuple-element.1057), channel_id=1, source_target_pairs={{0,1},{1,0},{2,3},{3,2},{4,5},{5,4},{6,7},{7,6},{8,9},{9,8},{10,11... | collective-permute-start | bytes 491528 | tf_op jit(solution)/shard_map/ppermute | solution.py:396
  19.0 10.2 %collective-permute-start.51 = (bf16[640,128]{1,0:T(8,128)(2,1)}, bf16[640,128]{1,0:T(8,128)(2,1)S(1)}, u32[]{:S(2)}, u32[]{:S(2)}) collective-permute-start(bf16[640,128]{1,0:T(8,128)(2,1)} %get-tuple-element.1058), channel_id=1, source_target_pairs={{1,2},{2,1},{3,4},{4,3},{5,6},{6,5},{9,10},{10,9},{11,12},{12,11},... | collective-permute-start | bytes 491528 | tf_op jit(solution)/shard_map/ppermute | solution.py:397
  20.9 3.7 %copy-start.16 = (s32[16,128]{1,0:T(8,128)S(1)}, s32[16,128]{1,0:T(8,128)}, u32[]{:S(2)}) copy-start(s32[16,128]{1,0:T(8,128)} %param.56) | copy-start | bytes 24580
  24.6 4.6 %copy-start = (bf16[3,800,200]{1,2,0:T(8,128)(2,1)S(1)}, bf16[3,800,200]{1,2,0:T(8,128)(2,1)}, u32[]{:S(2)}) copy-start(bf16[3,800,200]{1,2,0:T(8,128)(2,1)} %param.61) | copy-start | bytes 2880004
  24.7 1.5 %collective-permute-start.15 = (bf16[640,128]{1,0:T(8,128)(2,1)}, bf16[640,128]{1,0:T(8,128)(2,1)}, u32[]{:S(2)}, u32[]{:S(2)}) collective-permute-start(bf16[640,128]{1,0:T(8,128)(2,1)} %get-tuple-element.782), channel_id=1, source_target_pairs={{7,127},{15,119},{23,111},{31,103},{39,95},{47,87},{55,79},{63,71}... | collective-permute-start | bytes 491528 | tf_op jit(solution)/shard_map/cond/branch_15_fun/ppermute | solution.py:382
  29.2 10.3 %copy-start.3 = (bf16[3,200,800]{2,1,0:T(8,128)(2,1)S(1)}, bf16[3,200,800]{2,1,0:T(8,128)(2,1)}, u32[]{:S(2)}) copy-start(bf16[3,200,800]{2,1,0:T(8,128)(2,1)} %refs_1_.5) | copy-start | bytes 2880004
  29.2 10.3 %copy-start.5 = (bf16[3,200,7,7]{1,3,2,0:T(8,128)(2,1)S(1)}, bf16[3,200,7,7]{1,3,2,0:T(8,128)(2,1)}, u32[]{:S(2)}) copy-start(bf16[3,200,7,7]{1,3,2,0:T(8,128)(2,1)} %param.58) | copy-start | bytes 176404
  29.2 10.3 %copy-start.7 = (bf16[3,200]{1,0:T(4,128)(2,1)S(1)}, bf16[3,200]{1,0:T(4,128)(2,1)}, u32[]{:S(2)}) copy-start(bf16[3,200]{1,0:T(4,128)(2,1)} %refs_2_.5) | copy-start | bytes 3604
  35.6 20.0 %copy-start.11 = (bf16[200,16,128]{2,1,0:T(8,128)(2,1)}, bf16[200,16,128]{2,1,0:T(8,128)(2,1)S(1)}, u32[]{:S(2)}) copy-start(bf16[200,16,128]{2,1,0:T(8,128)(2,1)S(1)} %get-tuple-element.1063.x_ref.refs_0_) | copy-start | bytes 2457604
  35.6 7.6 %collective-permute-start.52 = (bf16[896,128]{1,0:T(8,128)(2,1)S(1)}, bf16[896,128]{1,0:T(8,128)(2,1)S(1)}, u32[]{:S(2)}, u32[]{:S(2)}) collective-permute-start(bf16[896,128]{1,0:T(8,128)(2,1)S(1)} %get-tuple-element.1064.send_ref), channel_id=1, source_target_pairs={{0,8},{8,16},{16,24},{24,32},{32,40},{40,48},{48,56},{56,64},{64,7... | collective-permute-start | bytes 688136 | tf_op jit(solution)/shard_map/ppermute | solution.py:392
  35.7 7.5 %collective-permute-start.53 = (bf16[896,128]{1,0:T(8,128)(2,1)S(1)}, bf16[896,128]{1,0:T(8,128)(2,1)S(1)}, u32[]{:S(2)}, u32[]{:S(2)}) collective-permute-start(bf16[896,128]{1,0:T(8,128)(2,1)S(1)} %get-tuple-element.1064.send_ref), channel_id=1, source_target_pairs={{8,0},{16,8},{24,16},{32,24},{40,32},{48,40},{56,48},{64,56},{72,6... | collective-permute-start | bytes 688136 | tf_op jit(solution)/shard_map/ppermute | solution.py:393
  42.2 13.4 %copy-start.8 = (bf16[25,48,336]{2,1,0:T(8,128)(2,1)}, bf16[25,48,336]{2,1,0:T(8,128)(2,1)S(1)}, u32[]{:S(2)}) copy-start(bf16[25,48,336]{2,1,0:T(8,128)(2,1)S(1)} %get-tuple-element.1069.refs_2_) | copy-start | bytes 2419204
  44.7 12.4 %collective-permute-start.54 = (bf16[640,128]{1,0:T(8,128)(2,1)S(1)}, bf16[640,128]{1,0:T(8,128)(2,1)S(1)}, u32[]{:S(2)}, u32[]{:S(2)}) collective-permute-start(bf16[640,128]{1,0:T(8,128)(2,1)S(1)} %get-tuple-element.1070), channel_id=1, source_target_pairs={{0,1},{1,0},{2,3},{3,2},{4,5},{5,4},{6,7},{7,6},{8,9},{9,8},{10,11... | collective-permute-start | bytes 491528 | tf_op jit(solution)/shard_map/ppermute | solution.py:396
  50.0 11.6 %collective-permute-start.55 = (bf16[640,128]{1,0:T(8,128)(2,1)}, bf16[640,128]{1,0:T(8,128)(2,1)S(1)}, u32[]{:S(2)}, u32[]{:S(2)}) collective-permute-start(bf16[640,128]{1,0:T(8,128)(2,1)} %get-tuple-element.1071), channel_id=1, source_target_pairs={{1,2},{2,1},{3,4},{4,3},{5,6},{6,5},{9,10},{10,9},{11,12},{12,11},... | collective-permute-start | bytes 491528 | tf_op jit(solution)/shard_map/ppermute | solution.py:397
  55.7 1.3 %collective-permute-start.31 = (bf16[640,128]{1,0:T(8,128)(2,1)}, bf16[640,128]{1,0:T(8,128)(2,1)}, u32[]{:S(2)}, u32[]{:S(2)}) collective-permute-start(bf16[640,128]{1,0:T(8,128)(2,1)} %get-tuple-element.894), channel_id=1, source_target_pairs={{7,127},{15,119},{23,111},{31,103},{39,95},{47,87},{55,79},{63,71}... | collective-permute-start | bytes 491528 | tf_op jit(solution)/shard_map/cond/branch_15_fun/ppermute | solution.py:382
  68.1 17.1 %copy-start.12 = (bf16[200,16,128]{2,1,0:T(8,128)(2,1)}, bf16[200,16,128]{2,1,0:T(8,128)(2,1)S(1)}, u32[]{:S(2)}) copy-start(bf16[200,16,128]{2,1,0:T(8,128)(2,1)S(1)} %get-tuple-element.1076.x_ref.refs_0_) | copy-start | bytes 2457604
  68.1 7.6 %collective-permute-start.56 = (bf16[896,128]{1,0:T(8,128)(2,1)S(1)}, bf16[896,128]{1,0:T(8,128)(2,1)S(1)}, u32[]{:S(2)}, u32[]{:S(2)}) collective-permute-start(bf16[896,128]{1,0:T(8,128)(2,1)S(1)} %get-tuple-element.1077.send_ref), channel_id=1, source_target_pairs={{0,8},{8,16},{16,24},{24,32},{32,40},{40,48},{48,56},{56,64},{64,7... | collective-permute-start | bytes 688136 | tf_op jit(solution)/shard_map/ppermute | solution.py:392
  68.2 7.5 %collective-permute-start.57 = (bf16[896,128]{1,0:T(8,128)(2,1)S(1)}, bf16[896,128]{1,0:T(8,128)(2,1)S(1)}, u32[]{:S(2)}, u32[]{:S(2)}) collective-permute-start(bf16[896,128]{1,0:T(8,128)(2,1)S(1)} %get-tuple-element.1077.send_ref), channel_id=1, source_target_pairs={{8,0},{16,8},{24,16},{32,24},{40,32},{48,40},{56,48},{64,56},{72,6... | collective-permute-start | bytes 688136 | tf_op jit(solution)/shard_map/ppermute | solution.py:393
  74.7 10.4 %copy-start.9 = (bf16[25,48,336]{2,1,0:T(8,128)(2,1)}, bf16[25,48,336]{2,1,0:T(8,128)(2,1)S(1)}, u32[]{:S(2)}) copy-start(bf16[25,48,336]{2,1,0:T(8,128)(2,1)S(1)} %get-tuple-element.1082.refs_2_) | copy-start | bytes 2419204
  74.7 10.4 %copy-start.14 = (bf16[800,200]{1,0:T(8,128)(2,1)}, bf16[800,200]{1,0:T(8,128)(2,1)S(1)}, u32[]{:S(2)}) copy-start(bf16[800,200]{1,0:T(8,128)(2,1)S(1)} %get-tuple-element.1085.refs_6_) | copy-start | bytes 960004
  77.4 9.2 %collective-permute-start.58 = (bf16[640,128]{1,0:T(8,128)(2,1)S(1)}, bf16[640,128]{1,0:T(8,128)(2,1)S(1)}, u32[]{:S(2)}, u32[]{:S(2)}) collective-permute-start(bf16[640,128]{1,0:T(8,128)(2,1)S(1)} %get-tuple-element.1083), channel_id=1, source_target_pairs={{0,1},{1,0},{2,3},{3,2},{4,5},{5,4},{6,7},{7,6},{8,9},{9,8},{10,11... | collective-permute-start | bytes 491528 | tf_op jit(solution)/shard_map/ppermute | solution.py:396
  80.2 10.8 %collective-permute-start.59 = (bf16[640,128]{1,0:T(8,128)(2,1)}, bf16[640,128]{1,0:T(8,128)(2,1)S(1)}, u32[]{:S(2)}, u32[]{:S(2)}) collective-permute-start(bf16[640,128]{1,0:T(8,128)(2,1)} %get-tuple-element.1084), channel_id=1, source_target_pairs={{1,2},{2,1},{3,4},{4,3},{5,6},{6,5},{9,10},{10,9},{11,12},{12,11},... | collective-permute-start | bytes 491528 | tf_op jit(solution)/shard_map/ppermute | solution.py:397
  85.2 1.3 %collective-permute-start.47 = (bf16[640,128]{1,0:T(8,128)(2,1)}, bf16[640,128]{1,0:T(8,128)(2,1)}, u32[]{:S(2)}, u32[]{:S(2)}) collective-permute-start(bf16[640,128]{1,0:T(8,128)(2,1)} %get-tuple-element.1006), channel_id=1, source_target_pairs={{7,127},{15,119},{23,111},{31,103},{39,95},{47,87},{55,79},{63,71}... | collective-permute-start | bytes 491528 | tf_op jit(solution)/shard_map/cond/branch_15_fun/ppermute | solution.py:382
where the time goes:
time: 98.3 us; the launch traced here: 97.7 us
  Pallas kernels  44.3 us (45%)
  starting transfers between devices  34.1 us (35%)
  waiting for transfers between devices  13.9 us (14%)
  local copies, waits for them, and re-layouts  4.06 us (4%)
  between operations  1.19 us (1%)
    pallas_call x3, Pallas kernels, run_block(): pl.pallas_call(lambda *refs: block_kernel(last, block, *refs), out_shape=...  19.4 us
    ppermute x3, starting transfers between devices, local(): r1 = lax.ppermute(q1, 'merid', even_pairs)  12.4 us
    ppermute x3, waiting for transfers between devices, local(): r2 = lax.ppermute(q2, 'merid', odd_pairs)  12 us
    ppermute x3, starting transfers between devices, local(): lax.ppermute(send, 'zonal', [((z + 1) % zonal, z) for z in range(zonal)])  11.6 us
    pallas_call x3, Pallas kernels, conv_own(): pl.pallas_call(conv_kernel, out_shape=jax.ShapeDtypeStruct((ROWS, GROUPS,...  10.4 us
    pallas_call x3, Pallas kernels, make_bands(): pl.pallas_call(lambda *refs: band_kernel(block, *refs), out_shape=(jax.Sh...  8.17 us
    ppermute x3, starting transfers between devices, local(): r2 = lax.ppermute(q2, 'merid', odd_pairs)  5.72 us
    pallas_call x3, Pallas kernels, turn_edges(): pl.pallas_call(turn_kernel, out_shape=(jax.ShapeDtypeStruct((SWAP, LANES)...  4.63 us
  transfers between devices with their start and end apart: 15, of which 5 were waited for; matrix products, arithmetic and copies ran while one was open for 1% of the time, Pallas kernels for 19%

commit v1 on v0

--- a/solution.py
+++ b/solution.py
@@ -337,11 +337,13 @@
         return (x_ref[pl.ds(first, count)].astype(F32) + o) * mask[None]
 
     if last:
-        def finish(g, carry):
-            out_ref[pl.ds(8 * g, 8)] = tile(pl.multiple_of(8 * g, 8), 8).astype(BF16)
-            return carry
-
-        lax.fori_loop(0, GROUPS, finish, 0)
+        whole = edge_refs[0]
+        for g in range(GROUPS):
+            whole[8 * g : 8 * g + 8] = tile(8 * g, 8).astype(BF16)
+            if g % 5 == 4:
+                part = pl.ds(8 * (g - 4), 40)
+                pltpu.make_async_copy(whole.at[part], out_ref.at[part], sem).start()
+        pltpu.make_async_copy(whole, out_ref, sem).wait()
     else:
         emit_edges(tile, o_ref, out_ref, *edge_refs)
 
@@ -353,8 +355,9 @@
         lambda *refs: block_kernel(last, block, *refs),
         out_shape=shapes,
         in_specs=[VM, ANY] + [VM] * 8,
-        out_specs=(VM,) * len(shapes),
-        scratch_shapes=[
+        out_specs=(ANY,) if last else (VM,) * len(shapes),
+        scratch_shapes=([pltpu.VMEM((C, ROWS, LANES), BF16)] if last else [])
+        + [
             pltpu.VMEM((6, GROUPS, 8, LANES), F32),
             pltpu.VMEM((6, GROUPS, 8, LANES), F32),
             pltpu.VMEM((6, GROUPS, 8, LANES), F32),

time: 98.3 us -> 96.2 us (0.979)
  waiting for transfers between devices: 13.9 us -> 11.9 us
    ppermute x3, waiting for transfers between devices: 12 us -> 9.98 us  [local(): r2 = lax.ppermute(q2, 'merid', odd_pairs)]
    ppermute x3, starting transfers between devices: 12.4 us -> 11 us  [local(): r1 = lax.ppermute(q1, 'merid', even_pairs)]
    ppermute x3, starting transfers between devices: 5.72 us -> 6.71 us  [local(): r2 = lax.ppermute(q2, 'merid', odd_pairs)]
  transfers between devices with their start and end apart: 15 -> 15, of which waited for: 5 -> 5; matrix products, arithmetic and copies ran while one was open for 1% -> 1% of each run, Pallas kernels for 19% -> 20%
where the time goes in v1:
time: 96.2 us; the launch traced here: 94.9 us
  Pallas kernels  44 us (46%)
  starting transfers between devices  33.7 us (35%)
  waiting for transfers between devices  11.9 us (12%)
  local copies, waits for them, and re-layouts  4.06 us (4%)
  between operations  1.18 us (1%)
    pallas_call x3, Pallas kernels, run_block(): pl.pallas_call(lambda *refs: block_kernel(last, block, *refs), out_shape=...  19.1 us
    ppermute x3, starting transfers between devices, local(): lax.ppermute(send, 'zonal', [((z + 1) % zonal, z) for z in range(zonal)])  11.5 us
    ppermute x3, starting transfers between devices, local(): r1 = lax.ppermute(q1, 'merid', even_pairs)  11 us
    pallas_call x3, Pallas kernels, conv_own(): pl.pallas_call(conv_kernel, out_shape=jax.ShapeDtypeStruct((ROWS, GROUPS,...  10.4 us
    ppermute x3, waiting for transfers between devices, local(): r2 = lax.ppermute(q2, 'merid', odd_pairs)  9.98 us
    pallas_call x3, Pallas kernels, make_bands(): pl.pallas_call(lambda *refs: band_kernel(block, *refs), out_shape=(jax.Sh...  8.16 us
    ppermute x3, starting transfers between devices, local(): r2 = lax.ppermute(q2, 'merid', odd_pairs)  6.71 us
    pallas_call x3, Pallas kernels, turn_edges(): pl.pallas_call(turn_kernel, out_shape=(jax.ShapeDtypeStruct((SWAP, LANES)...  4.63 us
  transfers between devices with their start and end apart: 15, of which 5 were waited for; matrix products, arithmetic and copies ran while one was open for 1% of the time, Pallas kernels for 20%

profile of v1, /device:TPU:6, one launch (start us, length us, event | category | flops | bytes accessed | tf_op | source)
XLA Modules:
  0.0 94.9 jit_solution(15431662245073107048)
XLA Ops:
  0.0 1.7 %shard_map.73 = (bf16[896,128]{1,0:T(8,128)(2,1)S(1)}, bf16[608,128]{1,0:T(8,128)(2,1)S(1)}) custom-call(bf16[200,16,128]{2,1,0:T(8,128)(2,1)} %refs_0_.1), custom_call_target="tpu_custom_call" | custom-call | tf_op jit(solution)/shard_map/pallas_call | solution.py:156
  1.8 3.9 %collective-permute-start.49 = (bf16[896,128]{1,0:T(8,128)(2,1)S(1)}, bf16[896,128]{1,0:T(8,128)(2,1)S(1)}, u32[]{:S(2)}, u32[]{:S(2)}) collective-permute-start(bf16[896,128]{1,0:T(8,128)(2,1)S(1)} %get-tuple-element.1051.send_ref), channel_id=1, source_target_pairs={{8,0},{16,8},{24,16},{32,24},{40,32},{48,40},{56,48},{64,56},{72,6... | collective-permute-start | bytes 688136 | tf_op jit(solution)/shard_map/ppermute | solution.py:396
  7.6 1.2 %copy-done.2 = bf16[3,200,800]{2,1,0:T(8,128)(2,1)S(1)} copy-done((bf16[3,200,800]{2,1,0:T(8,128)(2,1)S(1)}, bf16[3,200,800]{2,1,0:T(8,128)(2,1)}, u32[]{:S(2)}) %copy-start.2) | copy-done | bytes 960024
  10.4 2.7 %shard_map.75 = (bf16[25,128,896]{2,1,0:T(8,128)(2,1)S(1)}, bf16[25,48,336]{2,1,0:T(8,128)(2,1)S(1)}, bf16[800,200]{1,0:T(8,128)(2,1)S(1)}, f32[200,128]{1,0:T(8,128)S(1)}) custom-call(bf16[3,7,7,200]{3,2,1,0:T(8,128)(2,1)S(1)} %bitcast.6, bf16[3,200,800]{2,1,0:T(8,128)(2,1)S(1)} %copy-done.2, bf16[3,200]{1,0:T(4,128)(2,1)S(1)} %copy-done.6), custom_call_target="tpu_custom_call" | custom-call | flops 2147483648 | bytes 9000000 | tf_op jit(solution)/shard_map/pallas_call | solution.py:97
  13.2 1.5 %shard_map.74 = (bf16[640,128]{1,0:T(8,128)(2,1)S(1)}, bf16[640,128]{1,0:T(8,128)(2,1)}) custom-call(s32[2048]{0:T(1024)S(1)} %copy-done.1, bf16[896,128]{1,0:T(8,128)(2,1)S(1)} %collective-permute-done.48.west_ref, bf16[896,128]{1,0:T(8,128)(2,1)S(1)} %collective-permute-done.49.east_ref, bf16[896,128]{1,0:T(8,128)(2,1)S(1)} %get-tuple-element.1051.send_ref, ...), custom_call_target="tpu_custom_call" | custom-call | tf_op jit(solution)/shard_map/pallas_call | solution.py:214
  14.6 4.3 %collective-permute-start.50 = (bf16[640,128]{1,0:T(8,128)(2,1)S(1)}, bf16[640,128]{1,0:T(8,128)(2,1)S(1)}, u32[]{:S(2)}, u32[]{:S(2)}) collective-permute-start(bf16[640,128]{1,0:T(8,128)(2,1)S(1)} %get-tuple-element.1057), channel_id=1, source_target_pairs={{0,1},{1,0},{2,3},{3,2},{4,5},{5,4},{6,7},{7,6},{8,9},{9,8},{10,11... | collective-permute-start | bytes 491528 | tf_op jit(solution)/shard_map/ppermute | solution.py:399
  19.0 1.9 %collective-permute-start.51 = (bf16[640,128]{1,0:T(8,128)(2,1)}, bf16[640,128]{1,0:T(8,128)(2,1)S(1)}, u32[]{:S(2)}, u32[]{:S(2)}) collective-permute-start(bf16[640,128]{1,0:T(8,128)(2,1)} %get-tuple-element.1058), channel_id=1, source_target_pairs={{1,2},{2,1},{3,4},{4,3},{5,6},{6,5},{9,10},{10,9},{11,12},{12,11},... | collective-permute-start | bytes 491528 | tf_op jit(solution)/shard_map/ppermute | solution.py:400
  20.9 3.7 %shard_map.76.refs_1_ = f32[16,25,8,128]{3,2,1,0:T(8,128)} custom-call(bf16[200,16,128]{2,1,0:T(8,128)(2,1)S(1)} %copy-done.10, bf16[25,128,896]{2,1,0:T(8,128)(2,1)S(1)} %get-tuple-element.1054.band_ref, bf16[896,128]{1,0:T(8,128)(2,1)S(1)} %collective-permute-done.48.west_ref, bf16[896,128]{1,0:T(8,128)(2,1)S(1)} %collective-permute-done.49.east_ref), custom_call_target="tpu_custom_call" | custom-call | flops 3355443200 | bytes 9000000 | tf_op jit(solution)/shard_map/pallas_call | solution.py:264
  24.6 1.5 %conditional.3 = (bf16[640,128]{1,0:T(8,128)(2,1)}, f32[16,128]{1,0:T(8,128)S(1)}) conditional(s32[]{:T(128)} %clamp.2, (bf16[640,128]{1,0:T(8,128)(2,1)}, s32[16,128]{1,0:T(8,128)S(1)}, bf16[200,16,128]{2,1,0:T(8,128)(2,1)S(1)}, f32[16,25,8,128]{3,2,1,0:T(8,128)}, bf16[25,48,336]{2,1,0:T(8,128)(2,1)S(1)}, ...), branch_computations={%region_0.1_spmd, %region_1.2_spmd, %region_2.3_spmd, %region_3.4_... | conditional | bytes 655416 | solution.py:403
  24.7 1.5 %collective-permute-start.1 = (bf16[640,128]{1,0:T(8,128)(2,1)}, bf16[640,128]{1,0:T(8,128)(2,1)}, u32[]{:S(2)}, u32[]{:S(2)}) collective-permute-start(bf16[640,128]{1,0:T(8,128)(2,1)} %get-tuple-element.684), channel_id=1, source_target_pairs={{7,15},{15,7},{23,127},{31,119},{39,111},{47,103},{55,95},{63,87},... | collective-permute-start | bytes 491528 | tf_op jit(solution)/shard_map/cond/branch_1_fun/ppermute | solution.py:385
  26.1 2.6 %collective-permute-done.51.refs_4_ = bf16[640,128]{1,0:T(8,128)(2,1)S(1)} collective-permute-done((bf16[640,128]{1,0:T(8,128)(2,1)}, bf16[640,128]{1,0:T(8,128)(2,1)S(1)}, u32[]{:S(2)}, u32[]{:S(2)}) %collective-permute-start.51) | collective-permute-done | bytes 163872 | tf_op jit(solution)/shard_map/ppermute | solution.py:400
  28.8 6.4 %shard_map.77 = (bf16[200,16,128]{2,1,0:T(8,128)(2,1)S(1)}, bf16[896,128]{1,0:T(8,128)(2,1)S(1)}, bf16[608,128]{1,0:T(8,128)(2,1)S(1)}) custom-call(bf16[200,16,128]{2,1,0:T(8,128)(2,1)} %refs_0_.1, f32[16,25,8,128]{3,2,1,0:T(8,128)} %shard_map.76.refs_1_, bf16[25,48,336]{2,1,0:T(8,128)(2,1)S(1)} %get-tuple-element.1056.refs_2_, ...), custom_call_target="tpu_custom_call" | custom-call | tf_op jit(solution)/shard_map/pallas_call | solution.py:354
  35.3 3.8 %collective-permute-start.53 = (bf16[896,128]{1,0:T(8,128)(2,1)S(1)}, bf16[896,128]{1,0:T(8,128)(2,1)S(1)}, u32[]{:S(2)}, u32[]{:S(2)}) collective-permute-start(bf16[896,128]{1,0:T(8,128)(2,1)S(1)} %get-tuple-element.1064.send_ref), channel_id=1, source_target_pairs={{8,0},{16,8},{24,16},{32,24},{40,32},{48,40},{56,48},{64,56},{72,6... | collective-permute-start | bytes 688136 | tf_op jit(solution)/shard_map/ppermute | solution.py:396
  39.1 2.7 %shard_map.79 = (bf16[25,128,896]{2,1,0:T(8,128)(2,1)S(1)}, bf16[25,48,336]{2,1,0:T(8,128)(2,1)S(1)}, bf16[800,200]{1,0:T(8,128)(2,1)S(1)}, f32[200,128]{1,0:T(8,128)S(1)}) custom-call(bf16[3,7,7,200]{3,2,1,0:T(8,128)(2,1)S(1)} %bitcast.7, bf16[3,200,800]{2,1,0:T(8,128)(2,1)S(1)} %copy-done.3, bf16[3,200]{1,0:T(4,128)(2,1)S(1)} %copy-done.7), custom_call_target="tpu_custom_call" | custom-call | flops 2147483648 | bytes 9000000 | tf_op jit(solution)/shard_map/pallas_call | solution.py:97
  42.8 1.5 %shard_map.78 = (bf16[640,128]{1,0:T(8,128)(2,1)S(1)}, bf16[640,128]{1,0:T(8,128)(2,1)}) custom-call(s32[2048]{0:T(1024)S(1)} %copy-done.1, bf16[896,128]{1,0:T(8,128)(2,1)S(1)} %collective-permute-done.52.west_ref, bf16[896,128]{1,0:T(8,128)(2,1)S(1)} %collective-permute-done.53.east_ref, bf16[896,128]{1,0:T(8,128)(2,1)S(1)} %get-tuple-element.1064.send_ref, ...), custom_call_target="tpu_custom_call" | custom-call | tf_op jit(solution)/shard_map/pallas_call | solution.py:214
  44.3 2.3 %collective-permute-start.54 = (bf16[640,128]{1,0:T(8,128)(2,1)S(1)}, bf16[640,128]{1,0:T(8,128)(2,1)S(1)}, u32[]{:S(2)}, u32[]{:S(2)}) collective-permute-start(bf16[640,128]{1,0:T(8,128)(2,1)S(1)} %get-tuple-element.1070), channel_id=1, source_target_pairs={{0,1},{1,0},{2,3},{3,2},{4,5},{5,4},{6,7},{7,6},{8,9},{9,8},{10,11... | collective-permute-start | bytes 491528 | tf_op jit(solution)/shard_map/ppermute | solution.py:399
  46.6 2.9 %collective-permute-start.55 = (bf16[640,128]{1,0:T(8,128)(2,1)}, bf16[640,128]{1,0:T(8,128)(2,1)S(1)}, u32[]{:S(2)}, u32[]{:S(2)}) collective-permute-start(bf16[640,128]{1,0:T(8,128)(2,1)} %get-tuple-element.1071), channel_id=1, source_target_pairs={{1,2},{2,1},{3,4},{4,3},{5,6},{6,5},{9,10},{10,9},{11,12},{12,11},... | collective-permute-start | bytes 491528 | tf_op jit(solution)/shard_map/ppermute | solution.py:400
  49.5 3.6 %shard_map.80.refs_1_ = f32[16,25,8,128]{3,2,1,0:T(8,128)} custom-call(bf16[200,16,128]{2,1,0:T(8,128)(2,1)S(1)} %get-tuple-element.1063.x_ref.refs_0_, bf16[25,128,896]{2,1,0:T(8,128)(2,1)S(1)} %get-tuple-element.1067.band_ref, bf16[896,128]{1,0:T(8,128)(2,1)S(1)} %collective-permute-done.52.west_ref, bf16[896,128]{1,0:T(8,128)(2,1)S(1)} %collective-permute-done.53.east_ref), custom_call_target="tpu_custom_call" | custom-call | flops 3355443200 | bytes 9000000 | tf_op jit(solution)/shard_map/pallas_call | solution.py:264
  53.2 1.4 %conditional.4 = (bf16[640,128]{1,0:T(8,128)(2,1)}, f32[16,128]{1,0:T(8,128)S(1)}) conditional(s32[]{:T(128)} %clamp.2, (bf16[640,128]{1,0:T(8,128)(2,1)}, s32[16,128]{1,0:T(8,128)S(1)}, bf16[200,16,128]{2,1,0:T(8,128)(2,1)S(1)}, f32[16,25,8,128]{3,2,1,0:T(8,128)}, bf16[25,48,336]{2,1,0:T(8,128)(2,1)S(1)}, ...), branch_computations={%region_16.17_spmd, %region_17.18_spmd, %region_18.19_spmd, %regio... | conditional | bytes 655416 | solution.py:403
  53.2 1.3 %collective-permute-start.17 = (bf16[640,128]{1,0:T(8,128)(2,1)}, bf16[640,128]{1,0:T(8,128)(2,1)}, u32[]{:S(2)}, u32[]{:S(2)}) collective-permute-start(bf16[640,128]{1,0:T(8,128)(2,1)} %get-tuple-element.796), channel_id=1, source_target_pairs={{7,15},{15,7},{23,127},{31,119},{39,111},{47,103},{55,95},{63,87},... | collective-permute-start | bytes 491528 | tf_op jit(solution)/shard_map/cond/branch_1_fun/ppermute | solution.py:385
  54.5 3.4 %collective-permute-done.55.refs_4_ = bf16[640,128]{1,0:T(8,128)(2,1)S(1)} collective-permute-done((bf16[640,128]{1,0:T(8,128)(2,1)}, bf16[640,128]{1,0:T(8,128)(2,1)S(1)}, u32[]{:S(2)}, u32[]{:S(2)}) %collective-permute-start.55) | collective-permute-done | bytes 163872 | tf_op jit(solution)/shard_map/ppermute | solution.py:400
  58.0 6.5 %shard_map.81 = (bf16[200,16,128]{2,1,0:T(8,128)(2,1)S(1)}, bf16[896,128]{1,0:T(8,128)(2,1)S(1)}, bf16[608,128]{1,0:T(8,128)(2,1)S(1)}) custom-call(bf16[200,16,128]{2,1,0:T(8,128)(2,1)} %copy-done.11, f32[16,25,8,128]{3,2,1,0:T(8,128)} %shard_map.80.refs_1_, bf16[25,48,336]{2,1,0:T(8,128)(2,1)} %copy-done.8, ...), custom_call_target="tpu_custom_call" | custom-call | tf_op jit(solution)/shard_map/pallas_call | solution.py:354
  64.6 3.7 %collective-permute-start.57 = (bf16[896,128]{1,0:T(8,128)(2,1)S(1)}, bf16[896,128]{1,0:T(8,128)(2,1)S(1)}, u32[]{:S(2)}, u32[]{:S(2)}) collective-permute-start(bf16[896,128]{1,0:T(8,128)(2,1)S(1)} %get-tuple-element.1077.send_ref), channel_id=1, source_target_pairs={{8,0},{16,8},{24,16},{32,24},{40,32},{48,40},{56,48},{64,56},{72,6... | collective-permute-start | bytes 688136 | tf_op jit(solution)/shard_map/ppermute | solution.py:396
  68.4 2.7 %shard_map.83 = (bf16[25,128,896]{2,1,0:T(8,128)(2,1)S(1)}, bf16[25,48,336]{2,1,0:T(8,128)(2,1)S(1)}, bf16[800,200]{1,0:T(8,128)(2,1)S(1)}, f32[200,128]{1,0:T(8,128)S(1)}) custom-call(bf16[3,7,7,200]{3,2,1,0:T(8,128)(2,1)S(1)} %bitcast.8, bf16[3,200,800]{2,1,0:T(8,128)(2,1)S(1)} %copy-done.3, bf16[3,200]{1,0:T(4,128)(2,1)S(1)} %copy-done.7), custom_call_target="tpu_custom_call" | custom-call | flops 2147483648 | bytes 9000000 | tf_op jit(solution)/shard_map/pallas_call | solution.py:97
  72.1 1.7 %shard_map.82 = (bf16[640,128]{1,0:T(8,128)(2,1)S(1)}, bf16[640,128]{1,0:T(8,128)(2,1)}) custom-call(s32[2048]{0:T(1024)S(1)} %copy-done.1, bf16[896,128]{1,0:T(8,128)(2,1)S(1)} %collective-permute-done.56.west_ref, bf16[896,128]{1,0:T(8,128)(2,1)S(1)} %collective-permute-done.57.east_ref, bf16[896,128]{1,0:T(8,128)(2,1)S(1)} %get-tuple-element.1077.send_ref, ...), custom_call_target="tpu_custom_call" | custom-call | tf_op jit(solution)/shard_map/pallas_call | solution.py:214
  73.8 4.4 %collective-permute-start.58 = (bf16[640,128]{1,0:T(8,128)(2,1)S(1)}, bf16[640,128]{1,0:T(8,128)(2,1)S(1)}, u32[]{:S(2)}, u32[]{:S(2)}) collective-permute-start(bf16[640,128]{1,0:T(8,128)(2,1)S(1)} %get-tuple-element.1083), channel_id=1, source_target_pairs={{0,1},{1,0},{2,3},{3,2},{4,5},{5,4},{6,7},{7,6},{8,9},{9,8},{10,11... | collective-permute-start | bytes 491528 | tf_op jit(solution)/shard_map/ppermute | solution.py:399
  78.2 1.9 %collective-permute-start.59 = (bf16[640,128]{1,0:T(8,128)(2,1)}, bf16[640,128]{1,0:T(8,128)(2,1)S(1)}, u32[]{:S(2)}, u32[]{:S(2)}) collective-permute-start(bf16[640,128]{1,0:T(8,128)(2,1)} %get-tuple-element.1084), channel_id=1, source_target_pairs={{1,2},{2,1},{3,4},{4,3},{5,6},{6,5},{9,10},{10,9},{11,12},{12,11},... | collective-permute-start | bytes 491528 | tf_op jit(solution)/shard_map/ppermute | solution.py:400
  80.1 3.0 %shard_map.84.refs_1_ = f32[16,25,8,128]{3,2,1,0:T(8,128)S(1)} custom-call(bf16[200,16,128]{2,1,0:T(8,128)(2,1)S(1)} %get-tuple-element.1076.x_ref.refs_0_, bf16[25,128,896]{2,1,0:T(8,128)(2,1)S(1)} %get-tuple-element.1080.band_ref, bf16[896,128]{1,0:T(8,128)(2,1)S(1)} %collective-permute-done.56.west_ref, bf16[896,128]{1,0:T(8,128)(2,1)S(1)} %collective-permute-done.57.east_ref), custom_call_target="tpu_custom_call" | custom-call | flops 3355443200 | bytes 9000000 | tf_op jit(solution)/shard_map/pallas_call | solution.py:264
  83.1 1.4 %conditional.5 = (bf16[640,128]{1,0:T(8,128)(2,1)}, f32[16,128]{1,0:T(8,128)S(1)}) conditional(s32[]{:T(128)} %clamp.2, (bf16[640,128]{1,0:T(8,128)(2,1)}, s32[16,128]{1,0:T(8,128)S(1)}, bf16[200,16,128]{2,1,0:T(8,128)(2,1)S(1)}, f32[16,25,8,128]{3,2,1,0:T(8,128)S(1)}, bf16[25,48,336]{2,1,0:T(8,128)(2,1)S(1)}, ...), branch_computations={%region_32.33_spmd, %region_33.34_spmd, %region_34.35_spmd, %regio... | conditional | bytes 655416 | solution.py:403
  83.2 1.3 %collective-permute-start.33 = (bf16[640,128]{1,0:T(8,128)(2,1)}, bf16[640,128]{1,0:T(8,128)(2,1)}, u32[]{:S(2)}, u32[]{:S(2)}) collective-permute-start(bf16[640,128]{1,0:T(8,128)(2,1)} %get-tuple-element.908), channel_id=1, source_target_pairs={{7,15},{15,7},{23,127},{31,119},{39,111},{47,103},{55,95},{63,87},... | collective-permute-start | bytes 491528 | tf_op jit(solution)/shard_map/cond/branch_1_fun/ppermute | solution.py:385
  84.5 3.9 %collective-permute-done.59.refs_4_ = bf16[640,128]{1,0:T(8,128)(2,1)S(1)} collective-permute-done((bf16[640,128]{1,0:T(8,128)(2,1)}, bf16[640,128]{1,0:T(8,128)(2,1)S(1)}, u32[]{:S(2)}, u32[]{:S(2)}) %collective-permute-start.59) | collective-permute-done | bytes 163872 | tf_op jit(solution)/shard_map/ppermute | solution.py:400
  88.5 6.3 %shard_map.85 = bf16[200,16,128]{2,1,0:T(8,128)(2,1)} custom-call(bf16[200,16,128]{2,1,0:T(8,128)(2,1)} %copy-done.12, f32[16,25,8,128]{3,2,1,0:T(8,128)S(1)} %shard_map.84.refs_1_, bf16[25,48,336]{2,1,0:T(8,128)(2,1)} %copy-done.9, bf16[640,128]{1,0:T(8,128)(2,1)S(1)} %collective-permute-done.58.refs_3_, ...), custom_call_target="tpu_custom_call" | custom-call | tf_op jit(solution)/shard_map/pallas_call | solution.py:354
  (52 shorter events, 5.1 us)
Async XLA Ops:
  1.7 11.4 %collective-permute-start.48 = (bf16[896,128]{1,0:T(8,128)(2,1)S(1)}, bf16[896,128]{1,0:T(8,128)(2,1)S(1)}, u32[]{:S(2)}, u32[]{:S(2)}) collective-permute-start(bf16[896,128]{1,0:T(8,128)(2,1)S(1)} %get-tuple-element.1051.send_ref), channel_id=1, source_target_pairs={{0,8},{8,16},{16,24},{24,32},{32,40},{40,48},{48,56},{56,64},{64,7... | collective-permute-start | bytes 688136 | tf_op jit(solution)/shard_map/ppermute | solution.py:395
  1.8 11.3 %collective-permute-start.49 = (bf16[896,128]{1,0:T(8,128)(2,1)S(1)}, bf16[896,128]{1,0:T(8,128)(2,1)S(1)}, u32[]{:S(2)}, u32[]{:S(2)}) collective-permute-start(bf16[896,128]{1,0:T(8,128)(2,1)S(1)} %get-tuple-element.1051.send_ref), channel_id=1, source_target_pairs={{8,0},{16,8},{24,16},{32,24},{40,32},{48,40},{56,48},{64,56},{72,6... | collective-permute-start | bytes 688136 | tf_op jit(solution)/shard_map/ppermute | solution.py:396
  7.6 1.2 %copy-start.2 = (bf16[3,200,800]{2,1,0:T(8,128)(2,1)S(1)}, bf16[3,200,800]{2,1,0:T(8,128)(2,1)}, u32[]{:S(2)}) copy-start(bf16[3,200,800]{2,1,0:T(8,128)(2,1)} %refs_1_.5) | copy-start | bytes 2880004
  8.8 0.9 copy-start.4
  9.7 0.7 copy-start.6
  10.4 2.8 %copy-start.1 = (s32[2048]{0:T(1024)S(1)}, s32[2048]{0:T(1024)}, u32[]{:S(2)}) copy-start(s32[2048]{0:T(1024)} %fold_ref.5) | copy-start | bytes 24580
  10.4 10.5 %copy-start.10 = (bf16[200,16,128]{2,1,0:T(8,128)(2,1)S(1)}, bf16[200,16,128]{2,1,0:T(8,128)(2,1)}, u32[]{:S(2)}) copy-start(bf16[200,16,128]{2,1,0:T(8,128)(2,1)} %refs_0_.1) | copy-start | bytes 2457604
  13.1 11.5 %copy-start.13 = (bf16[800,200]{1,0:T(8,128)(2,1)}, bf16[800,200]{1,0:T(8,128)(2,1)S(1)}, u32[]{:S(2)}) copy-start(bf16[800,200]{1,0:T(8,128)(2,1)S(1)} %get-tuple-element.1059.refs_6_) | copy-start | bytes 960004
  13.1 11.5 %copy-start.15 = (f32[200,128]{1,0:T(8,128)}, f32[200,128]{1,0:T(8,128)S(1)}, u32[]{:S(2)}) copy-start(f32[200,128]{1,0:T(8,128)S(1)} %get-tuple-element.1060.refs_8_) | copy-start | bytes 307204
  14.6 11.5 %collective-permute-start.50 = (bf16[640,128]{1,0:T(8,128)(2,1)S(1)}, bf16[640,128]{1,0:T(8,128)(2,1)S(1)}, u32[]{:S(2)}, u32[]{:S(2)}) collective-permute-start(bf16[640,128]{1,0:T(8,128)(2,1)S(1)} %get-tuple-element.1057), channel_id=1, source_target_pairs={{0,1},{1,0},{2,3},{3,2},{4,5},{5,4},{6,7},{7,6},{8,9},{9,8},{10,11... | collective-permute-start | bytes 491528 | tf_op jit(solution)/shard_map/ppermute | solution.py:399
  19.0 9.8 %collective-permute-start.51 = (bf16[640,128]{1,0:T(8,128)(2,1)}, bf16[640,128]{1,0:T(8,128)(2,1)S(1)}, u32[]{:S(2)}, u32[]{:S(2)}) collective-permute-start(bf16[640,128]{1,0:T(8,128)(2,1)} %get-tuple-element.1058), channel_id=1, source_target_pairs={{1,2},{2,1},{3,4},{4,3},{5,6},{6,5},{9,10},{10,9},{11,12},{12,11},... | collective-permute-start | bytes 491528 | tf_op jit(solution)/shard_map/ppermute | solution.py:400
  20.9 3.7 %copy-start.16 = (s32[16,128]{1,0:T(8,128)S(1)}, s32[16,128]{1,0:T(8,128)}, u32[]{:S(2)}) copy-start(s32[16,128]{1,0:T(8,128)} %param.56) | copy-start | bytes 24580
  24.6 4.2 %copy-start = (bf16[3,800,200]{1,2,0:T(8,128)(2,1)S(1)}, bf16[3,800,200]{1,2,0:T(8,128)(2,1)}, u32[]{:S(2)}) copy-start(bf16[3,800,200]{1,2,0:T(8,128)(2,1)} %param.61) | copy-start | bytes 2880004
  24.7 1.5 %collective-permute-start.1 = (bf16[640,128]{1,0:T(8,128)(2,1)}, bf16[640,128]{1,0:T(8,128)(2,1)}, u32[]{:S(2)}, u32[]{:S(2)}) collective-permute-start(bf16[640,128]{1,0:T(8,128)(2,1)} %get-tuple-element.684), channel_id=1, source_target_pairs={{7,15},{15,7},{23,127},{31,119},{39,111},{47,103},{55,95},{63,87},... | collective-permute-start | bytes 491528 | tf_op jit(solution)/shard_map/cond/branch_1_fun/ppermute | solution.py:385
  28.8 10.3 %copy-start.3 = (bf16[3,200,800]{2,1,0:T(8,128)(2,1)S(1)}, bf16[3,200,800]{2,1,0:T(8,128)(2,1)}, u32[]{:S(2)}) copy-start(bf16[3,200,800]{2,1,0:T(8,128)(2,1)} %refs_1_.5) | copy-start | bytes 2880004
  28.8 10.3 %copy-start.5 = (bf16[3,200,7,7]{1,3,2,0:T(8,128)(2,1)S(1)}, bf16[3,200,7,7]{1,3,2,0:T(8,128)(2,1)}, u32[]{:S(2)}) copy-start(bf16[3,200,7,7]{1,3,2,0:T(8,128)(2,1)} %param.58) | copy-start | bytes 176404
  28.8 10.3 %copy-start.7 = (bf16[3,200]{1,0:T(4,128)(2,1)S(1)}, bf16[3,200]{1,0:T(4,128)(2,1)}, u32[]{:S(2)}) copy-start(bf16[3,200]{1,0:T(4,128)(2,1)} %refs_2_.5) | copy-start | bytes 3604
  35.2 18.0 %copy-start.11 = (bf16[200,16,128]{2,1,0:T(8,128)(2,1)}, bf16[200,16,128]{2,1,0:T(8,128)(2,1)S(1)}, u32[]{:S(2)}) copy-start(bf16[200,16,128]{2,1,0:T(8,128)(2,1)S(1)} %get-tuple-element.1063.x_ref.refs_0_) | copy-start | bytes 2457604
  35.2 7.6 %collective-permute-start.52 = (bf16[896,128]{1,0:T(8,128)(2,1)S(1)}, bf16[896,128]{1,0:T(8,128)(2,1)S(1)}, u32[]{:S(2)}, u32[]{:S(2)}) collective-permute-start(bf16[896,128]{1,0:T(8,128)(2,1)S(1)} %get-tuple-element.1064.send_ref), channel_id=1, source_target_pairs={{0,8},{8,16},{16,24},{24,32},{32,40},{40,48},{48,56},{56,64},{64,7... | collective-permute-start | bytes 688136 | tf_op jit(solution)/shard_map/ppermute | solution.py:395
  35.3 7.5 %collective-permute-start.53 = (bf16[896,128]{1,0:T(8,128)(2,1)S(1)}, bf16[896,128]{1,0:T(8,128)(2,1)S(1)}, u32[]{:S(2)}, u32[]{:S(2)}) collective-permute-start(bf16[896,128]{1,0:T(8,128)(2,1)S(1)} %get-tuple-element.1064.send_ref), channel_id=1, source_target_pairs={{8,0},{16,8},{24,16},{32,24},{40,32},{48,40},{56,48},{64,56},{72,6... | collective-permute-start | bytes 688136 | tf_op jit(solution)/shard_map/ppermute | solution.py:396
  41.8 11.3 %copy-start.8 = (bf16[25,48,336]{2,1,0:T(8,128)(2,1)}, bf16[25,48,336]{2,1,0:T(8,128)(2,1)S(1)}, u32[]{:S(2)}) copy-start(bf16[25,48,336]{2,1,0:T(8,128)(2,1)S(1)} %get-tuple-element.1069.refs_2_) | copy-start | bytes 2419204
  44.3 10.3 %collective-permute-start.54 = (bf16[640,128]{1,0:T(8,128)(2,1)S(1)}, bf16[640,128]{1,0:T(8,128)(2,1)S(1)}, u32[]{:S(2)}, u32[]{:S(2)}) collective-permute-start(bf16[640,128]{1,0:T(8,128)(2,1)S(1)} %get-tuple-element.1070), channel_id=1, source_target_pairs={{0,1},{1,0},{2,3},{3,2},{4,5},{5,4},{6,7},{7,6},{8,9},{9,8},{10,11... | collective-permute-start | bytes 491528 | tf_op jit(solution)/shard_map/ppermute | solution.py:399
  46.6 11.4 %collective-permute-start.55 = (bf16[640,128]{1,0:T(8,128)(2,1)}, bf16[640,128]{1,0:T(8,128)(2,1)S(1)}, u32[]{:S(2)}, u32[]{:S(2)}) collective-permute-start(bf16[640,128]{1,0:T(8,128)(2,1)} %get-tuple-element.1071), channel_id=1, source_target_pairs={{1,2},{2,1},{3,4},{4,3},{5,6},{6,5},{9,10},{10,9},{11,12},{12,11},... | collective-permute-start | bytes 491528 | tf_op jit(solution)/shard_map/ppermute | solution.py:400
  53.2 1.3 %collective-permute-start.17 = (bf16[640,128]{1,0:T(8,128)(2,1)}, bf16[640,128]{1,0:T(8,128)(2,1)}, u32[]{:S(2)}, u32[]{:S(2)}) collective-permute-start(bf16[640,128]{1,0:T(8,128)(2,1)} %get-tuple-element.796), channel_id=1, source_target_pairs={{7,15},{15,7},{23,127},{31,119},{39,111},{47,103},{55,95},{63,87},... | collective-permute-start | bytes 491528 | tf_op jit(solution)/shard_map/cond/branch_1_fun/ppermute | solution.py:385
  64.4 18.7 %copy-start.12 = (bf16[200,16,128]{2,1,0:T(8,128)(2,1)}, bf16[200,16,128]{2,1,0:T(8,128)(2,1)S(1)}, u32[]{:S(2)}) copy-start(bf16[200,16,128]{2,1,0:T(8,128)(2,1)S(1)} %get-tuple-element.1076.x_ref.refs_0_) | copy-start | bytes 2457604
  64.4 7.6 %collective-permute-start.56 = (bf16[896,128]{1,0:T(8,128)(2,1)S(1)}, bf16[896,128]{1,0:T(8,128)(2,1)S(1)}, u32[]{:S(2)}, u32[]{:S(2)}) collective-permute-start(bf16[896,128]{1,0:T(8,128)(2,1)S(1)} %get-tuple-element.1077.send_ref), channel_id=1, source_target_pairs={{0,8},{8,16},{16,24},{24,32},{32,40},{40,48},{48,56},{56,64},{64,7... | collective-permute-start | bytes 688136 | tf_op jit(solution)/shard_map/ppermute | solution.py:395
  64.6 7.4 %collective-permute-start.57 = (bf16[896,128]{1,0:T(8,128)(2,1)S(1)}, bf16[896,128]{1,0:T(8,128)(2,1)S(1)}, u32[]{:S(2)}, u32[]{:S(2)}) collective-permute-start(bf16[896,128]{1,0:T(8,128)(2,1)S(1)} %get-tuple-element.1077.send_ref), channel_id=1, source_target_pairs={{8,0},{16,8},{24,16},{32,24},{40,32},{48,40},{56,48},{64,56},{72,6... | collective-permute-start | bytes 688136 | tf_op jit(solution)/shard_map/ppermute | solution.py:396
  71.1 12.0 %copy-start.9 = (bf16[25,48,336]{2,1,0:T(8,128)(2,1)}, bf16[25,48,336]{2,1,0:T(8,128)(2,1)S(1)}, u32[]{:S(2)}) copy-start(bf16[25,48,336]{2,1,0:T(8,128)(2,1)S(1)} %get-tuple-element.1082.refs_2_) | copy-start | bytes 2419204
  71.1 12.0 %copy-start.14 = (bf16[800,200]{1,0:T(8,128)(2,1)}, bf16[800,200]{1,0:T(8,128)(2,1)S(1)}, u32[]{:S(2)}) copy-start(bf16[800,200]{1,0:T(8,128)(2,1)S(1)} %get-tuple-element.1085.refs_6_) | copy-start | bytes 960004
  73.8 10.8 %collective-permute-start.58 = (bf16[640,128]{1,0:T(8,128)(2,1)S(1)}, bf16[640,128]{1,0:T(8,128)(2,1)S(1)}, u32[]{:S(2)}, u32[]{:S(2)}) collective-permute-start(bf16[640,128]{1,0:T(8,128)(2,1)S(1)} %get-tuple-element.1083), channel_id=1, source_target_pairs={{0,1},{1,0},{2,3},{3,2},{4,5},{5,4},{6,7},{7,6},{8,9},{9,8},{10,11... | collective-permute-start | bytes 491528 | tf_op jit(solution)/shard_map/ppermute | solution.py:399
  78.2 10.3 %collective-permute-start.59 = (bf16[640,128]{1,0:T(8,128)(2,1)}, bf16[640,128]{1,0:T(8,128)(2,1)S(1)}, u32[]{:S(2)}, u32[]{:S(2)}) collective-permute-start(bf16[640,128]{1,0:T(8,128)(2,1)} %get-tuple-element.1084), channel_id=1, source_target_pairs={{1,2},{2,1},{3,4},{4,3},{5,6},{6,5},{9,10},{10,9},{11,12},{12,11},... | collective-permute-start | bytes 491528 | tf_op jit(solution)/shard_map/ppermute | solution.py:400
  83.2 1.3 %collective-permute-start.33 = (bf16[640,128]{1,0:T(8,128)(2,1)}, bf16[640,128]{1,0:T(8,128)(2,1)}, u32[]{:S(2)}, u32[]{:S(2)}) collective-permute-start(bf16[640,128]{1,0:T(8,128)(2,1)} %get-tuple-element.908), channel_id=1, source_target_pairs={{7,15},{15,7},{23,127},{31,119},{39,111},{47,103},{55,95},{63,87},... | collective-permute-start | bytes 491528 | tf_op jit(solution)/shard_map/cond/branch_1_fun/ppermute | solution.py:385

commit v2 on v1

--- a/solution.py
+++ b/solution.py
@@ -73,7 +73,7 @@
         place(2 * p, 2 * p + 1, main_tap, own_main, main_ref, pl.multiple_of(16 * p, 16))
         return carry
 
-    lax.fori_loop(0, ROWS // 2, main_pair, 0, unroll=4)
+    lax.fori_loop(0, ROWS // 2, main_pair, 0, unroll=8)
     lane = lax.broadcasted_iota(jnp.int32, (1, 7 * SIDE), 1)
     e_side, slot = lane // SIDE, lane % SIDE
     k = slot // 8

time: 96.2 us -> 97.5 us (1.014)
  starting transfers between devices: 33.7 us -> 36 us
  Pallas kernels: 44 us -> 42.7 us
    ppermute x3, starting transfers between devices: 11 us -> 14.4 us  [local(): r1 = lax.ppermute(q1, 'merid', even_pairs)]
    pallas_call x3, Pallas kernels: 8.16 us -> 7.15 us  [make_bands(): pl.pallas_call(lambda *refs: band_kernel(block, *refs), out_shape=(jax.Sh...]
    ppermute x3, starting transfers between devices: 6.71 us -> 5.72 us  [local(): r2 = lax.ppermute(q2, 'merid', odd_pairs)]
  transfers between devices with their start and end apart: 15 -> 15, of which waited for: 5 -> 5; matrix products, arithmetic and copies ran while one was open for 1% -> 1% of each run, Pallas kernels for 20% -> 18%
where the time goes in v2:
time: 97.5 us; the launch traced here: 96 us
  Pallas kernels  42.7 us (44%)
  starting transfers between devices  36 us (37%)
  waiting for transfers between devices  11.8 us (12%)
  local copies, waits for them, and re-layouts  4.06 us (4%)
  between operations  1.19 us (1%)
    pallas_call x3, Pallas kernels, run_block(): pl.pallas_call(lambda *refs: block_kernel(last, block, *refs), out_shape=...  19.1 us
    ppermute x3, starting transfers between devices, local(): r1 = lax.ppermute(q1, 'merid', even_pairs)  14.4 us
    ppermute x3, starting transfers between devices, local(): lax.ppermute(send, 'zonal', [((z + 1) % zonal, z) for z in range(zonal)])  11.6 us
    pallas_call x3, Pallas kernels, conv_own(): pl.pallas_call(conv_kernel, out_shape=jax.ShapeDtypeStruct((ROWS, GROUPS,...  10.4 us
    ppermute x3, waiting for transfers between devices, local(): r2 = lax.ppermute(q2, 'merid', odd_pairs)  9.21 us
    pallas_call x3, Pallas kernels, make_bands(): pl.pallas_call(lambda *refs: band_kernel(block, *refs), out_shape=(jax.Sh...  7.15 us
    ppermute x3, starting transfers between devices, local(): r2 = lax.ppermute(q2, 'merid', odd_pairs)  5.72 us
    pallas_call x3, Pallas kernels, turn_edges(): pl.pallas_call(turn_kernel, out_shape=(jax.ShapeDtypeStruct((SWAP, LANES)...  4.41 us
  transfers between devices with their start and end apart: 15, of which 5 were waited for; matrix products, arithmetic and copies ran while one was open for 1% of the time, Pallas kernels for 18%

profile of v2, /device:TPU:6, one launch (start us, length us, event | category | flops | bytes accessed | tf_op | source)
XLA Modules:
  0.0 96.0 jit_solution(16360364505056086635)
XLA Ops:
  0.0 1.7 %shard_map.73 = (bf16[896,128]{1,0:T(8,128)(2,1)S(1)}, bf16[608,128]{1,0:T(8,128)(2,1)S(1)}) custom-call(bf16[200,16,128]{2,1,0:T(8,128)(2,1)} %refs_0_.1), custom_call_target="tpu_custom_call" | custom-call | tf_op jit(solution)/shard_map/pallas_call | solution.py:156
  1.8 3.9 %collective-permute-start.49 = (bf16[896,128]{1,0:T(8,128)(2,1)S(1)}, bf16[896,128]{1,0:T(8,128)(2,1)S(1)}, u32[]{:S(2)}, u32[]{:S(2)}) collective-permute-start(bf16[896,128]{1,0:T(8,128)(2,1)S(1)} %get-tuple-element.1051.send_ref), channel_id=1, source_target_pairs={{8,0},{16,8},{24,16},{32,24},{40,32},{48,40},{56,48},{64,56},{72,6... | collective-permute-start | bytes 688136 | tf_op jit(solution)/shard_map/ppermute | solution.py:396
  10.4 2.4 %shard_map.75 = (bf16[25,128,896]{2,1,0:T(8,128)(2,1)S(1)}, bf16[25,48,336]{2,1,0:T(8,128)(2,1)S(1)}, bf16[800,200]{1,0:T(8,128)(2,1)S(1)}, f32[200,128]{1,0:T(8,128)S(1)}) custom-call(bf16[3,7,7,200]{3,2,1,0:T(8,128)(2,1)S(1)} %bitcast.6, bf16[3,200,800]{2,1,0:T(8,128)(2,1)S(1)} %copy-done.2, bf16[3,200]{1,0:T(4,128)(2,1)S(1)} %copy-done.6), custom_call_target="tpu_custom_call" | custom-call | flops 2147483648 | bytes 9000000 | tf_op jit(solution)/shard_map/pallas_call | solution.py:97
  12.8 1.5 %shard_map.74 = (bf16[640,128]{1,0:T(8,128)(2,1)S(1)}, bf16[640,128]{1,0:T(8,128)(2,1)}) custom-call(s32[2048]{0:T(1024)S(1)} %copy-done.1, bf16[896,128]{1,0:T(8,128)(2,1)S(1)} %collective-permute-done.48.west_ref, bf16[896,128]{1,0:T(8,128)(2,1)S(1)} %collective-permute-done.49.east_ref, bf16[896,128]{1,0:T(8,128)(2,1)S(1)} %get-tuple-element.1051.send_ref, ...), custom_call_target="tpu_custom_call" | custom-call | tf_op jit(solution)/shard_map/pallas_call | solution.py:214
  14.3 4.3 %collective-permute-start.50 = (bf16[640,128]{1,0:T(8,128)(2,1)S(1)}, bf16[640,128]{1,0:T(8,128)(2,1)S(1)}, u32[]{:S(2)}, u32[]{:S(2)}) collective-permute-start(bf16[640,128]{1,0:T(8,128)(2,1)S(1)} %get-tuple-element.1057), channel_id=1, source_target_pairs={{0,1},{1,0},{2,3},{3,2},{4,5},{5,4},{6,7},{7,6},{8,9},{9,8},{10,11... | collective-permute-start | bytes 491528 | tf_op jit(solution)/shard_map/ppermute | solution.py:399
  18.6 1.9 %collective-permute-start.51 = (bf16[640,128]{1,0:T(8,128)(2,1)}, bf16[640,128]{1,0:T(8,128)(2,1)S(1)}, u32[]{:S(2)}, u32[]{:S(2)}) collective-permute-start(bf16[640,128]{1,0:T(8,128)(2,1)} %get-tuple-element.1058), channel_id=1, source_target_pairs={{1,2},{2,1},{3,4},{4,3},{5,6},{6,5},{9,10},{10,9},{11,12},{12,11},... | collective-permute-start | bytes 491528 | tf_op jit(solution)/shard_map/ppermute | solution.py:400
  20.6 3.7 %shard_map.76.refs_1_ = f32[16,25,8,128]{3,2,1,0:T(8,128)} custom-call(bf16[200,16,128]{2,1,0:T(8,128)(2,1)S(1)} %copy-done.10, bf16[25,128,896]{2,1,0:T(8,128)(2,1)S(1)} %get-tuple-element.1054.band_ref, bf16[896,128]{1,0:T(8,128)(2,1)S(1)} %collective-permute-done.48.west_ref, bf16[896,128]{1,0:T(8,128)(2,1)S(1)} %collective-permute-done.49.east_ref), custom_call_target="tpu_custom_call" | custom-call | flops 3355443200 | bytes 9000000 | tf_op jit(solution)/shard_map/pallas_call | solution.py:264
  24.3 1.5 %conditional.3 = (bf16[640,128]{1,0:T(8,128)(2,1)}, f32[16,128]{1,0:T(8,128)S(1)}) conditional(s32[]{:T(128)} %clamp.2, (bf16[640,128]{1,0:T(8,128)(2,1)}, s32[16,128]{1,0:T(8,128)S(1)}, bf16[200,16,128]{2,1,0:T(8,128)(2,1)S(1)}, f32[16,25,8,128]{3,2,1,0:T(8,128)}, bf16[25,48,336]{2,1,0:T(8,128)(2,1)S(1)}, ...), branch_computations={%region_0.1_spmd, %region_1.2_spmd, %region_2.3_spmd, %region_3.4_... | conditional | bytes 655416 | solution.py:403
  24.3 1.5 %collective-permute-start.9 = (bf16[640,128]{1,0:T(8,128)(2,1)}, bf16[640,128]{1,0:T(8,128)(2,1)}, u32[]{:S(2)}, u32[]{:S(2)}) collective-permute-start(bf16[640,128]{1,0:T(8,128)(2,1)} %get-tuple-element.740), channel_id=1, source_target_pairs={{7,79},{15,71},{23,63},{31,55},{39,47},{47,39},{55,31},{63,23},{71... | collective-permute-start | bytes 491528 | tf_op jit(solution)/shard_map/cond/branch_9_fun/ppermute | solution.py:385
  25.8 2.7 %collective-permute-done.51.refs_4_ = bf16[640,128]{1,0:T(8,128)(2,1)S(1)} collective-permute-done((bf16[640,128]{1,0:T(8,128)(2,1)}, bf16[640,128]{1,0:T(8,128)(2,1)S(1)}, u32[]{:S(2)}, u32[]{:S(2)}) %collective-permute-start.51) | collective-permute-done | bytes 163872 | tf_op jit(solution)/shard_map/ppermute | solution.py:400
  28.5 6.4 %shard_map.77 = (bf16[200,16,128]{2,1,0:T(8,128)(2,1)S(1)}, bf16[896,128]{1,0:T(8,128)(2,1)S(1)}, bf16[608,128]{1,0:T(8,128)(2,1)S(1)}) custom-call(bf16[200,16,128]{2,1,0:T(8,128)(2,1)} %refs_0_.1, f32[16,25,8,128]{3,2,1,0:T(8,128)} %shard_map.76.refs_1_, bf16[25,48,336]{2,1,0:T(8,128)(2,1)S(1)} %get-tuple-element.1056.refs_2_, ...), custom_call_target="tpu_custom_call" | custom-call | tf_op jit(solution)/shard_map/pallas_call | solution.py:354
  35.0 3.8 %collective-permute-start.53 = (bf16[896,128]{1,0:T(8,128)(2,1)S(1)}, bf16[896,128]{1,0:T(8,128)(2,1)S(1)}, u32[]{:S(2)}, u32[]{:S(2)}) collective-permute-start(bf16[896,128]{1,0:T(8,128)(2,1)S(1)} %get-tuple-element.1064.send_ref), channel_id=1, source_target_pairs={{8,0},{16,8},{24,16},{32,24},{40,32},{48,40},{56,48},{64,56},{72,6... | collective-permute-start | bytes 688136 | tf_op jit(solution)/shard_map/ppermute | solution.py:396
  38.9 2.4 %shard_map.79 = (bf16[25,128,896]{2,1,0:T(8,128)(2,1)S(1)}, bf16[25,48,336]{2,1,0:T(8,128)(2,1)S(1)}, bf16[800,200]{1,0:T(8,128)(2,1)S(1)}, f32[200,128]{1,0:T(8,128)S(1)}) custom-call(bf16[3,7,7,200]{3,2,1,0:T(8,128)(2,1)S(1)} %bitcast.7, bf16[3,200,800]{2,1,0:T(8,128)(2,1)S(1)} %copy-done.3, bf16[3,200]{1,0:T(4,128)(2,1)S(1)} %copy-done.7), custom_call_target="tpu_custom_call" | custom-call | flops 2147483648 | bytes 9000000 | tf_op jit(solution)/shard_map/pallas_call | solution.py:97
  41.3 1.3 %collective-permute-done.52.west_ref = bf16[896,128]{1,0:T(8,128)(2,1)S(1)} collective-permute-done((bf16[896,128]{1,0:T(8,128)(2,1)S(1)}, bf16[896,128]{1,0:T(8,128)(2,1)S(1)}, u32[]{:S(2)}, u32[]{:S(2)}) %collective-permute-start.52) | collective-permute-done | bytes 229408 | tf_op jit(solution)/shard_map/ppermute | solution.py:395
  42.6 1.5 %shard_map.78 = (bf16[640,128]{1,0:T(8,128)(2,1)S(1)}, bf16[640,128]{1,0:T(8,128)(2,1)}) custom-call(s32[2048]{0:T(1024)S(1)} %copy-done.1, bf16[896,128]{1,0:T(8,128)(2,1)S(1)} %collective-permute-done.52.west_ref, bf16[896,128]{1,0:T(8,128)(2,1)S(1)} %collective-permute-done.53.east_ref, bf16[896,128]{1,0:T(8,128)(2,1)S(1)} %get-tuple-element.1064.send_ref, ...), custom_call_target="tpu_custom_call" | custom-call | tf_op jit(solution)/shard_map/pallas_call | solution.py:214
  44.0 5.6 %collective-permute-start.54 = (bf16[640,128]{1,0:T(8,128)(2,1)S(1)}, bf16[640,128]{1,0:T(8,128)(2,1)S(1)}, u32[]{:S(2)}, u32[]{:S(2)}) collective-permute-start(bf16[640,128]{1,0:T(8,128)(2,1)S(1)} %get-tuple-element.1070), channel_id=1, source_target_pairs={{0,1},{1,0},{2,3},{3,2},{4,5},{5,4},{6,7},{7,6},{8,9},{9,8},{10,11... | collective-permute-start | bytes 491528 | tf_op jit(solution)/shard_map/ppermute | solution.py:399
  49.6 1.9 %collective-permute-start.55 = (bf16[640,128]{1,0:T(8,128)(2,1)}, bf16[640,128]{1,0:T(8,128)(2,1)S(1)}, u32[]{:S(2)}, u32[]{:S(2)}) collective-permute-start(bf16[640,128]{1,0:T(8,128)(2,1)} %get-tuple-element.1071), channel_id=1, source_target_pairs={{1,2},{2,1},{3,4},{4,3},{5,6},{6,5},{9,10},{10,9},{11,12},{12,11},... | collective-permute-start | bytes 491528 | tf_op jit(solution)/shard_map/ppermute | solution.py:400
  51.5 3.6 %shard_map.80.refs_1_ = f32[16,25,8,128]{3,2,1,0:T(8,128)} custom-call(bf16[200,16,128]{2,1,0:T(8,128)(2,1)S(1)} %get-tuple-element.1063.x_ref.refs_0_, bf16[25,128,896]{2,1,0:T(8,128)(2,1)S(1)} %get-tuple-element.1067.band_ref, bf16[896,128]{1,0:T(8,128)(2,1)S(1)} %collective-permute-done.52.west_ref, bf16[896,128]{1,0:T(8,128)(2,1)S(1)} %collective-permute-done.53.east_ref), custom_call_target="tpu_custom_call" | custom-call | flops 3355443200 | bytes 9000000 | tf_op jit(solution)/shard_map/pallas_call | solution.py:264
  55.2 1.4 %conditional.4 = (bf16[640,128]{1,0:T(8,128)(2,1)}, f32[16,128]{1,0:T(8,128)S(1)}) conditional(s32[]{:T(128)} %clamp.2, (bf16[640,128]{1,0:T(8,128)(2,1)}, s32[16,128]{1,0:T(8,128)S(1)}, bf16[200,16,128]{2,1,0:T(8,128)(2,1)S(1)}, f32[16,25,8,128]{3,2,1,0:T(8,128)}, bf16[25,48,336]{2,1,0:T(8,128)(2,1)S(1)}, ...), branch_computations={%region_16.17_spmd, %region_17.18_spmd, %region_18.19_spmd, %regio... | conditional | bytes 655416 | solution.py:403
  55.2 1.3 %collective-permute-start.25 = (bf16[640,128]{1,0:T(8,128)(2,1)}, bf16[640,128]{1,0:T(8,128)(2,1)}, u32[]{:S(2)}, u32[]{:S(2)}) collective-permute-start(bf16[640,128]{1,0:T(8,128)(2,1)} %get-tuple-element.852), channel_id=1, source_target_pairs={{7,79},{15,71},{23,63},{31,55},{39,47},{47,39},{55,31},{63,23},{71... | collective-permute-start | bytes 491528 | tf_op jit(solution)/shard_map/cond/branch_9_fun/ppermute | solution.py:385
  56.6 2.9 %collective-permute-done.55.refs_4_ = bf16[640,128]{1,0:T(8,128)(2,1)S(1)} collective-permute-done((bf16[640,128]{1,0:T(8,128)(2,1)}, bf16[640,128]{1,0:T(8,128)(2,1)S(1)}, u32[]{:S(2)}, u32[]{:S(2)}) %collective-permute-start.55) | collective-permute-done | bytes 163872 | tf_op jit(solution)/shard_map/ppermute | solution.py:400
  59.5 6.5 %shard_map.81 = (bf16[200,16,128]{2,1,0:T(8,128)(2,1)S(1)}, bf16[896,128]{1,0:T(8,128)(2,1)S(1)}, bf16[608,128]{1,0:T(8,128)(2,1)S(1)}) custom-call(bf16[200,16,128]{2,1,0:T(8,128)(2,1)} %copy-done.11, f32[16,25,8,128]{3,2,1,0:T(8,128)} %shard_map.80.refs_1_, bf16[25,48,336]{2,1,0:T(8,128)(2,1)} %copy-done.8, ...), custom_call_target="tpu_custom_call" | custom-call | tf_op jit(solution)/shard_map/pallas_call | solution.py:354
  66.1 3.8 %collective-permute-start.57 = (bf16[896,128]{1,0:T(8,128)(2,1)S(1)}, bf16[896,128]{1,0:T(8,128)(2,1)S(1)}, u32[]{:S(2)}, u32[]{:S(2)}) collective-permute-start(bf16[896,128]{1,0:T(8,128)(2,1)S(1)} %get-tuple-element.1077.send_ref), channel_id=1, source_target_pairs={{8,0},{16,8},{24,16},{32,24},{40,32},{48,40},{56,48},{64,56},{72,6... | collective-permute-start | bytes 688136 | tf_op jit(solution)/shard_map/ppermute | solution.py:396
  69.9 2.4 %shard_map.83 = (bf16[25,128,896]{2,1,0:T(8,128)(2,1)S(1)}, bf16[25,48,336]{2,1,0:T(8,128)(2,1)S(1)}, bf16[800,200]{1,0:T(8,128)(2,1)S(1)}, f32[200,128]{1,0:T(8,128)S(1)}) custom-call(bf16[3,7,7,200]{3,2,1,0:T(8,128)(2,1)S(1)} %bitcast.8, bf16[3,200,800]{2,1,0:T(8,128)(2,1)S(1)} %copy-done.3, bf16[3,200]{1,0:T(4,128)(2,1)S(1)} %copy-done.7), custom_call_target="tpu_custom_call" | custom-call | flops 2147483648 | bytes 9000000 | tf_op jit(solution)/shard_map/pallas_call | solution.py:97
  73.6 1.5 %shard_map.82 = (bf16[640,128]{1,0:T(8,128)(2,1)S(1)}, bf16[640,128]{1,0:T(8,128)(2,1)}) custom-call(s32[2048]{0:T(1024)S(1)} %copy-done.1, bf16[896,128]{1,0:T(8,128)(2,1)S(1)} %collective-permute-done.56.west_ref, bf16[896,128]{1,0:T(8,128)(2,1)S(1)} %collective-permute-done.57.east_ref, bf16[896,128]{1,0:T(8,128)(2,1)S(1)} %get-tuple-element.1077.send_ref, ...), custom_call_target="tpu_custom_call" | custom-call | tf_op jit(solution)/shard_map/pallas_call | solution.py:214
  75.1 4.5 %collective-permute-start.58 = (bf16[640,128]{1,0:T(8,128)(2,1)S(1)}, bf16[640,128]{1,0:T(8,128)(2,1)S(1)}, u32[]{:S(2)}, u32[]{:S(2)}) collective-permute-start(bf16[640,128]{1,0:T(8,128)(2,1)S(1)} %get-tuple-element.1083), channel_id=1, source_target_pairs={{0,1},{1,0},{2,3},{3,2},{4,5},{5,4},{6,7},{7,6},{8,9},{9,8},{10,11... | collective-permute-start | bytes 491528 | tf_op jit(solution)/shard_map/ppermute | solution.py:399
  79.6 1.9 %collective-permute-start.59 = (bf16[640,128]{1,0:T(8,128)(2,1)}, bf16[640,128]{1,0:T(8,128)(2,1)S(1)}, u32[]{:S(2)}, u32[]{:S(2)}) collective-permute-start(bf16[640,128]{1,0:T(8,128)(2,1)} %get-tuple-element.1084), channel_id=1, source_target_pairs={{1,2},{2,1},{3,4},{4,3},{5,6},{6,5},{9,10},{10,9},{11,12},{12,11},... | collective-permute-start | bytes 491528 | tf_op jit(solution)/shard_map/ppermute | solution.py:400
  81.5 3.0 %shard_map.84.refs_1_ = f32[16,25,8,128]{3,2,1,0:T(8,128)S(1)} custom-call(bf16[200,16,128]{2,1,0:T(8,128)(2,1)S(1)} %get-tuple-element.1076.x_ref.refs_0_, bf16[25,128,896]{2,1,0:T(8,128)(2,1)S(1)} %get-tuple-element.1080.band_ref, bf16[896,128]{1,0:T(8,128)(2,1)S(1)} %collective-permute-done.56.west_ref, bf16[896,128]{1,0:T(8,128)(2,1)S(1)} %collective-permute-done.57.east_ref), custom_call_target="tpu_custom_call" | custom-call | flops 3355443200 | bytes 9000000 | tf_op jit(solution)/shard_map/pallas_call | solution.py:264
  84.6 1.4 %conditional.5 = (bf16[640,128]{1,0:T(8,128)(2,1)}, f32[16,128]{1,0:T(8,128)S(1)}) conditional(s32[]{:T(128)} %clamp.2, (bf16[640,128]{1,0:T(8,128)(2,1)}, s32[16,128]{1,0:T(8,128)S(1)}, bf16[200,16,128]{2,1,0:T(8,128)(2,1)S(1)}, f32[16,25,8,128]{3,2,1,0:T(8,128)S(1)}, bf16[25,48,336]{2,1,0:T(8,128)(2,1)S(1)}, ...), branch_computations={%region_32.33_spmd, %region_33.34_spmd, %region_34.35_spmd, %regio... | conditional | bytes 655416 | solution.py:403
  84.6 1.3 %collective-permute-start.41 = (bf16[640,128]{1,0:T(8,128)(2,1)}, bf16[640,128]{1,0:T(8,128)(2,1)}, u32[]{:S(2)}, u32[]{:S(2)}) collective-permute-start(bf16[640,128]{1,0:T(8,128)(2,1)} %get-tuple-element.964), channel_id=1, source_target_pairs={{7,79},{15,71},{23,63},{31,55},{39,47},{47,39},{55,31},{63,23},{71... | collective-permute-start | bytes 491528 | tf_op jit(solution)/shard_map/cond/branch_9_fun/ppermute | solution.py:385
  86.0 3.5 %collective-permute-done.59.refs_4_ = bf16[640,128]{1,0:T(8,128)(2,1)S(1)} collective-permute-done((bf16[640,128]{1,0:T(8,128)(2,1)}, bf16[640,128]{1,0:T(8,128)(2,1)S(1)}, u32[]{:S(2)}, u32[]{:S(2)}) %collective-permute-start.59) | collective-permute-done | bytes 163872 | tf_op jit(solution)/shard_map/ppermute | solution.py:400
  89.5 6.3 %shard_map.85 = bf16[200,16,128]{2,1,0:T(8,128)(2,1)} custom-call(bf16[200,16,128]{2,1,0:T(8,128)(2,1)} %copy-done.12, f32[16,25,8,128]{3,2,1,0:T(8,128)S(1)} %shard_map.84.refs_1_, bf16[25,48,336]{2,1,0:T(8,128)(2,1)} %copy-done.9, bf16[640,128]{1,0:T(8,128)(2,1)S(1)} %collective-permute-done.58.refs_3_, ...), custom_call_target="tpu_custom_call" | custom-call | tf_op jit(solution)/shard_map/pallas_call | solution.py:354
  (52 shorter events, 5.6 us)
Async XLA Ops:
  1.7 11.1 %collective-permute-start.48 = (bf16[896,128]{1,0:T(8,128)(2,1)S(1)}, bf16[896,128]{1,0:T(8,128)(2,1)S(1)}, u32[]{:S(2)}, u32[]{:S(2)}) collective-permute-start(bf16[896,128]{1,0:T(8,128)(2,1)S(1)} %get-tuple-element.1051.send_ref), channel_id=1, source_target_pairs={{0,8},{8,16},{16,24},{24,32},{32,40},{40,48},{48,56},{56,64},{64,7... | collective-permute-start | bytes 688136 | tf_op jit(solution)/shard_map/ppermute | solution.py:395
  1.8 11.0 %collective-permute-start.49 = (bf16[896,128]{1,0:T(8,128)(2,1)S(1)}, bf16[896,128]{1,0:T(8,128)(2,1)S(1)}, u32[]{:S(2)}, u32[]{:S(2)}) collective-permute-start(bf16[896,128]{1,0:T(8,128)(2,1)S(1)} %get-tuple-element.1051.send_ref), channel_id=1, source_target_pairs={{8,0},{16,8},{24,16},{32,24},{40,32},{48,40},{56,48},{64,56},{72,6... | collective-permute-start | bytes 688136 | tf_op jit(solution)/shard_map/ppermute | solution.py:396
  7.6 1.2 %copy-start.2 = (bf16[3,200,800]{2,1,0:T(8,128)(2,1)S(1)}, bf16[3,200,800]{2,1,0:T(8,128)(2,1)}, u32[]{:S(2)}) copy-start(bf16[3,200,800]{2,1,0:T(8,128)(2,1)} %refs_1_.5) | copy-start | bytes 2880004
  8.8 0.9 copy-start.4
  9.7 0.7 copy-start.6
  10.4 2.4 %copy-start.1 = (s32[2048]{0:T(1024)S(1)}, s32[2048]{0:T(1024)}, u32[]{:S(2)}) copy-start(s32[2048]{0:T(1024)} %fold_ref.5) | copy-start | bytes 24580
  10.4 10.2 %copy-start.10 = (bf16[200,16,128]{2,1,0:T(8,128)(2,1)S(1)}, bf16[200,16,128]{2,1,0:T(8,128)(2,1)}, u32[]{:S(2)}) copy-start(bf16[200,16,128]{2,1,0:T(8,128)(2,1)} %refs_0_.1) | copy-start | bytes 2457604
  12.8 11.5 %copy-start.13 = (bf16[800,200]{1,0:T(8,128)(2,1)}, bf16[800,200]{1,0:T(8,128)(2,1)S(1)}, u32[]{:S(2)}) copy-start(bf16[800,200]{1,0:T(8,128)(2,1)S(1)} %get-tuple-element.1059.refs_6_) | copy-start | bytes 960004
  12.8 11.5 %copy-start.15 = (f32[200,128]{1,0:T(8,128)}, f32[200,128]{1,0:T(8,128)S(1)}, u32[]{:S(2)}) copy-start(f32[200,128]{1,0:T(8,128)S(1)} %get-tuple-element.1060.refs_8_) | copy-start | bytes 307204
  14.3 11.5 %collective-permute-start.50 = (bf16[640,128]{1,0:T(8,128)(2,1)S(1)}, bf16[640,128]{1,0:T(8,128)(2,1)S(1)}, u32[]{:S(2)}, u32[]{:S(2)}) collective-permute-start(bf16[640,128]{1,0:T(8,128)(2,1)S(1)} %get-tuple-element.1057), channel_id=1, source_target_pairs={{0,1},{1,0},{2,3},{3,2},{4,5},{5,4},{6,7},{7,6},{8,9},{9,8},{10,11... | collective-permute-start | bytes 491528 | tf_op jit(solution)/shard_map/ppermute | solution.py:399
  18.6 9.9 %collective-permute-start.51 = (bf16[640,128]{1,0:T(8,128)(2,1)}, bf16[640,128]{1,0:T(8,128)(2,1)S(1)}, u32[]{:S(2)}, u32[]{:S(2)}) collective-permute-start(bf16[640,128]{1,0:T(8,128)(2,1)} %get-tuple-element.1058), channel_id=1, source_target_pairs={{1,2},{2,1},{3,4},{4,3},{5,6},{6,5},{9,10},{10,9},{11,12},{12,11},... | collective-permute-start | bytes 491528 | tf_op jit(solution)/shard_map/ppermute | solution.py:400
  20.5 3.7 %copy-start.16 = (s32[16,128]{1,0:T(8,128)S(1)}, s32[16,128]{1,0:T(8,128)}, u32[]{:S(2)}) copy-start(s32[16,128]{1,0:T(8,128)} %param.56) | copy-start | bytes 24580
  24.3 4.3 %copy-start = (bf16[3,800,200]{1,2,0:T(8,128)(2,1)S(1)}, bf16[3,800,200]{1,2,0:T(8,128)(2,1)}, u32[]{:S(2)}) copy-start(bf16[3,800,200]{1,2,0:T(8,128)(2,1)} %param.61) | copy-start | bytes 2880004
  24.3 1.5 %collective-permute-start.9 = (bf16[640,128]{1,0:T(8,128)(2,1)}, bf16[640,128]{1,0:T(8,128)(2,1)}, u32[]{:S(2)}, u32[]{:S(2)}) collective-permute-start(bf16[640,128]{1,0:T(8,128)(2,1)} %get-tuple-element.740), channel_id=1, source_target_pairs={{7,79},{15,71},{23,63},{31,55},{39,47},{47,39},{55,31},{63,23},{71... | collective-permute-start | bytes 491528 | tf_op jit(solution)/shard_map/cond/branch_9_fun/ppermute | solution.py:385
  28.5 10.3 %copy-start.3 = (bf16[3,200,800]{2,1,0:T(8,128)(2,1)S(1)}, bf16[3,200,800]{2,1,0:T(8,128)(2,1)}, u32[]{:S(2)}) copy-start(bf16[3,200,800]{2,1,0:T(8,128)(2,1)} %refs_1_.5) | copy-start | bytes 2880004
  28.5 10.3 %copy-start.5 = (bf16[3,200,7,7]{1,3,2,0:T(8,128)(2,1)S(1)}, bf16[3,200,7,7]{1,3,2,0:T(8,128)(2,1)}, u32[]{:S(2)}) copy-start(bf16[3,200,7,7]{1,3,2,0:T(8,128)(2,1)} %param.58) | copy-start | bytes 176404
  28.5 10.3 %copy-start.7 = (bf16[3,200]{1,0:T(4,128)(2,1)S(1)}, bf16[3,200]{1,0:T(4,128)(2,1)}, u32[]{:S(2)}) copy-start(bf16[3,200]{1,0:T(4,128)(2,1)} %refs_2_.5) | copy-start | bytes 3604
  34.9 20.2 %copy-start.11 = (bf16[200,16,128]{2,1,0:T(8,128)(2,1)}, bf16[200,16,128]{2,1,0:T(8,128)(2,1)S(1)}, u32[]{:S(2)}) copy-start(bf16[200,16,128]{2,1,0:T(8,128)(2,1)S(1)} %get-tuple-element.1063.x_ref.refs_0_) | copy-start | bytes 2457604
  34.9 7.6 %collective-permute-start.52 = (bf16[896,128]{1,0:T(8,128)(2,1)S(1)}, bf16[896,128]{1,0:T(8,128)(2,1)S(1)}, u32[]{:S(2)}, u32[]{:S(2)}) collective-permute-start(bf16[896,128]{1,0:T(8,128)(2,1)S(1)} %get-tuple-element.1064.send_ref), channel_id=1, source_target_pairs={{0,8},{8,16},{16,24},{24,32},{32,40},{40,48},{48,56},{56,64},{64,7... | collective-permute-start | bytes 688136 | tf_op jit(solution)/shard_map/ppermute | solution.py:395
  35.0 7.5 %collective-permute-start.53 = (bf16[896,128]{1,0:T(8,128)(2,1)S(1)}, bf16[896,128]{1,0:T(8,128)(2,1)S(1)}, u32[]{:S(2)}, u32[]{:S(2)}) collective-permute-start(bf16[896,128]{1,0:T(8,128)(2,1)S(1)} %get-tuple-element.1064.send_ref), channel_id=1, source_target_pairs={{8,0},{16,8},{24,16},{32,24},{40,32},{48,40},{56,48},{64,56},{72,6... | collective-permute-start | bytes 688136 | tf_op jit(solution)/shard_map/ppermute | solution.py:396
  41.3 13.9 %copy-start.8 = (bf16[25,48,336]{2,1,0:T(8,128)(2,1)}, bf16[25,48,336]{2,1,0:T(8,128)(2,1)S(1)}, u32[]{:S(2)}) copy-start(bf16[25,48,336]{2,1,0:T(8,128)(2,1)S(1)} %get-tuple-element.1069.refs_2_) | copy-start | bytes 2419204
  44.0 12.5 %collective-permute-start.54 = (bf16[640,128]{1,0:T(8,128)(2,1)S(1)}, bf16[640,128]{1,0:T(8,128)(2,1)S(1)}, u32[]{:S(2)}, u32[]{:S(2)}) collective-permute-start(bf16[640,128]{1,0:T(8,128)(2,1)S(1)} %get-tuple-element.1070), channel_id=1, source_target_pairs={{0,1},{1,0},{2,3},{3,2},{4,5},{5,4},{6,7},{7,6},{8,9},{9,8},{10,11... | collective-permute-start | bytes 491528 | tf_op jit(solution)/shard_map/ppermute | solution.py:399
  49.6 9.9 %collective-permute-start.55 = (bf16[640,128]{1,0:T(8,128)(2,1)}, bf16[640,128]{1,0:T(8,128)(2,1)S(1)}, u32[]{:S(2)}, u32[]{:S(2)}) collective-permute-start(bf16[640,128]{1,0:T(8,128)(2,1)} %get-tuple-element.1071), channel_id=1, source_target_pairs={{1,2},{2,1},{3,4},{4,3},{5,6},{6,5},{9,10},{10,9},{11,12},{12,11},... | collective-permute-start | bytes 491528 | tf_op jit(solution)/shard_map/ppermute | solution.py:400
  55.2 1.3 %collective-permute-start.25 = (bf16[640,128]{1,0:T(8,128)(2,1)}, bf16[640,128]{1,0:T(8,128)(2,1)}, u32[]{:S(2)}, u32[]{:S(2)}) collective-permute-start(bf16[640,128]{1,0:T(8,128)(2,1)} %get-tuple-element.852), channel_id=1, source_target_pairs={{7,79},{15,71},{23,63},{31,55},{39,47},{47,39},{55,31},{63,23},{71... | collective-permute-start | bytes 491528 | tf_op jit(solution)/shard_map/cond/branch_9_fun/ppermute | solution.py:385
  66.0 18.6 %copy-start.12 = (bf16[200,16,128]{2,1,0:T(8,128)(2,1)}, bf16[200,16,128]{2,1,0:T(8,128)(2,1)S(1)}, u32[]{:S(2)}) copy-start(bf16[200,16,128]{2,1,0:T(8,128)(2,1)S(1)} %get-tuple-element.1076.x_ref.refs_0_) | copy-start | bytes 2457604
  66.0 7.6 %collective-permute-start.56 = (bf16[896,128]{1,0:T(8,128)(2,1)S(1)}, bf16[896,128]{1,0:T(8,128)(2,1)S(1)}, u32[]{:S(2)}, u32[]{:S(2)}) collective-permute-start(bf16[896,128]{1,0:T(8,128)(2,1)S(1)} %get-tuple-element.1077.send_ref), channel_id=1, source_target_pairs={{0,8},{8,16},{16,24},{24,32},{32,40},{40,48},{48,56},{56,64},{64,7... | collective-permute-start | bytes 688136 | tf_op jit(solution)/shard_map/ppermute | solution.py:395
  66.1 7.5 %collective-permute-start.57 = (bf16[896,128]{1,0:T(8,128)(2,1)S(1)}, bf16[896,128]{1,0:T(8,128)(2,1)S(1)}, u32[]{:S(2)}, u32[]{:S(2)}) collective-permute-start(bf16[896,128]{1,0:T(8,128)(2,1)S(1)} %get-tuple-element.1077.send_ref), channel_id=1, source_target_pairs={{8,0},{16,8},{24,16},{32,24},{40,32},{48,40},{56,48},{64,56},{72,6... | collective-permute-start | bytes 688136 | tf_op jit(solution)/shard_map/ppermute | solution.py:396
  72.3 12.3 %copy-start.9 = (bf16[25,48,336]{2,1,0:T(8,128)(2,1)}, bf16[25,48,336]{2,1,0:T(8,128)(2,1)S(1)}, u32[]{:S(2)}) copy-start(bf16[25,48,336]{2,1,0:T(8,128)(2,1)S(1)} %get-tuple-element.1082.refs_2_) | copy-start | bytes 2419204
  72.3 12.3 %copy-start.14 = (bf16[800,200]{1,0:T(8,128)(2,1)}, bf16[800,200]{1,0:T(8,128)(2,1)S(1)}, u32[]{:S(2)}) copy-start(bf16[800,200]{1,0:T(8,128)(2,1)S(1)} %get-tuple-element.1085.refs_6_) | copy-start | bytes 960004
  75.1 10.9 %collective-permute-start.58 = (bf16[640,128]{1,0:T(8,128)(2,1)S(1)}, bf16[640,128]{1,0:T(8,128)(2,1)S(1)}, u32[]{:S(2)}, u32[]{:S(2)}) collective-permute-start(bf16[640,128]{1,0:T(8,128)(2,1)S(1)} %get-tuple-element.1083), channel_id=1, source_target_pairs={{0,1},{1,0},{2,3},{3,2},{4,5},{5,4},{6,7},{7,6},{8,9},{9,8},{10,11... | collective-permute-start | bytes 491528 | tf_op jit(solution)/shard_map/ppermute | solution.py:399
  79.6 9.9 %collective-permute-start.59 = (bf16[640,128]{1,0:T(8,128)(2,1)}, bf16[640,128]{1,0:T(8,128)(2,1)S(1)}, u32[]{:S(2)}, u32[]{:S(2)}) collective-permute-start(bf16[640,128]{1,0:T(8,128)(2,1)} %get-tuple-element.1084), channel_id=1, source_target_pairs={{1,2},{2,1},{3,4},{4,3},{5,6},{6,5},{9,10},{10,9},{11,12},{12,11},... | collective-permute-start | bytes 491528 | tf_op jit(solution)/shard_map/ppermute | solution.py:400
  84.6 1.3 %collective-permute-start.41 = (bf16[640,128]{1,0:T(8,128)(2,1)}, bf16[640,128]{1,0:T(8,128)(2,1)}, u32[]{:S(2)}, u32[]{:S(2)}) collective-permute-start(bf16[640,128]{1,0:T(8,128)(2,1)} %get-tuple-element.964), channel_id=1, source_target_pairs={{7,79},{15,71},{23,63},{31,55},{39,47},{47,39},{55,31},{63,23},{71... | collective-permute-start | bytes 491528 | tf_op jit(solution)/shard_map/cond/branch_9_fun/ppermute | solution.py:385
